TPU v7x, 32 devices: a whole 2x2x4 slice. The times are simulated.
32 devices in a mesh: grp: 4 (over y, x), ctx: 8 (over z, core).
Axes of the slice: x: 2, y: 2, z: 4, core: 2. Of those that a mesh axis runs over, the one named last changes fastest.
Arguments:
- query_raw: bfloat16 [8192, 256], P(('grp', 'ctx')), may hold values from -6 to 6
- key_raw: bfloat16 [8192, 256], P(('grp', 'ctx')), may hold values from -6 to 6
- values: bfloat16 [8192, 256], P(('grp', 'ctx')), may hold values from -6 to 6
- band_reach: int32 [64], P(('grp', 'ctx')), may hold values from 1 to 2, as said below
- partners: int32 [64, 4], P(('grp', 'ctx')), may hold values from 0 to 63, as said below
- gain_query: float32 [2, 128], replicated, may hold values from 0.5 to 2
- gain_key: float32 [2, 128], replicated, may hold values from 0.5 to 2
- cotangent: bfloat16 [8192, 256], P(('grp', 'ctx')), may hold values from -6 to 6
Outputs:
- output: bfloat16 [8192, 256], P(('grp', 'ctx'))
- grad_query: bfloat16 [8192, 256], P(('grp', 'ctx'))
- grad_key: bfloat16 [8192, 256], P(('grp', 'ctx'))
- grad_value: bfloat16 [8192, 256], P(('grp', 'ctx'))
Inputs may be any that keep to these rules, and one draw needn't show every extreme that they name: `band_reach`: some query block has reach 2. partners[b, l] is a block of the device whose index is (b // 2) xor (32 // 2**(l+1)).
All inputs are finite; a program needn't handle non-finite values.
Results may differ from a plain program's by a relative error of at most 0.0099.
Values may be sent and summed in bfloat16 or wider, within the bound.
A program may use at most 64 MiB of HBM per device.

v0:
```python
import jax
import jax.numpy as jnp
from jax import lax
from jax.sharding import PartitionSpec as P

HEADS = 2
BLOCK = 128
BAND = 2
LEVELS = 4


epsilon = 1e-05


def with_halo(cells, sides, width):
    for axis, dim in sides:
        count = lax.axis_size(axis)
        ends = count - 1
        head = lax.slice_in_dim(cells, 0, width, axis=dim)
        tail = lax.slice_in_dim(cells, cells.shape[dim] - width, cells.shape[dim], axis=dim)
        cells = jnp.concatenate(
            [
                lax.ppermute(tail, axis, [(i, (i + 1) % count) for i in range(ends)]),
                cells,
                lax.ppermute(head, axis, [((i + 1) % count, i) for i in range(ends)]),
            ],
            axis=dim,
        )
    return cells


def partner(value, axis, apart):
    mask = 2**apart
    pairs = [(source, source ^ mask) for source in range(lax.axis_size(axis))]
    return lax.ppermute(value, axis, pairs)


def from_behind(x, axis, by):
    devices = lax.axis_size(axis)
    pairs = [(i, i + by) for i in range(devices) if 0 <= i + by < devices]
    return lax.ppermute(x, axis, pairs)


def layer_norm(inputs, gain_row):
    average = jnp.mean(inputs, axis=-1, keepdims=True)
    centred = inputs - average
    inverse = lax.rsqrt(jnp.mean(centred * centred, axis=-1, keepdims=True) + epsilon)
    normed = centred * inverse
    return (normed, inverse, normed * gain_row)


def norm_back(upstream, normed, inverse, gain_row):
    scaled = upstream * gain_row
    first = jnp.mean(scaled, axis=-1, keepdims=True)
    second = jnp.mean(scaled * normed, axis=-1, keepdims=True)
    return (scaled - first - normed * second) * inverse


def body(query_raw, key_raw, values, band_reach, partners, gain_query, gain_key, cotangent):
    row_count, row_width = query_raw.shape
    head_dim = row_width // HEADS
    blocks = row_count // BLOCK
    block_extent = 2 * BAND + 1
    score_scale = head_dim ** (-0.5)
    shard_count = lax.axis_size(("grp", "ctx"))
    device = lax.axis_index(("grp", "ctx"))
    top_bit = shard_count.bit_length() - 1
    q_normed, q_inverse, q_scaled = layer_norm(
        query_raw.astype(jnp.float32).reshape(row_count, HEADS, head_dim), gain_query
    )
    k_normed, k_inverse, k_scaled = layer_norm(
        key_raw.astype(jnp.float32).reshape(row_count, HEADS, head_dim), gain_key
    )
    query_low = q_scaled.astype(jnp.bfloat16).reshape(row_count, row_width)
    key_low = k_scaled.astype(jnp.bfloat16).reshape(row_count, row_width)
    paired = jnp.stack((key_low, values))
    padded = with_halo(paired, ((("grp", "ctx"), 1),), BAND * BLOCK)
    padded = padded.reshape(2, blocks + 2 * BAND, BLOCK, row_width)
    band_sets = jnp.stack(
        [padded[:, offset : offset + blocks] for offset in range(block_extent)], axis=2
    )
    level_order = list(range(LEVELS))
    fetched = {}
    local_picks = {}
    for level_index in level_order:
        bit_number = top_bit - 1 - level_index
        partner_device = jnp.bitwise_xor(device, 1 << bit_number)
        received = partner(paired, ("grp", "ctx"), bit_number).reshape(2, blocks, BLOCK, row_width)
        local_picks[level_index] = partners[:, level_index] - partner_device * blocks
        fetched[level_index] = jnp.take(received, local_picks[level_index], axis=1)
    partner_sets = jnp.stack([fetched[level_index] for level_index in range(LEVELS)], axis=2)
    key_sets = jnp.concatenate((band_sets, partner_sets), axis=2)
    pick_table = jnp.stack([local_picks[level_index] for level_index in range(LEVELS)], axis=1)
    offsets = jnp.arange(block_extent, dtype=jnp.int32) - BAND
    block_ids = device * blocks + jnp.arange(blocks, dtype=jnp.int32)
    target = block_ids[:, None] + offsets[None, :]
    band_ok = (
        (jnp.abs(offsets)[None, :] <= band_reach[:, None])
        & (target >= 0)
        & (target < shard_count * blocks)
    )
    usable = jnp.concatenate((band_ok, jnp.ones((blocks, LEVELS), dtype=jnp.bool_)), axis=1)
    allowed = usable[:, None, :, None]
    slots = jnp.arange(blocks, dtype=jnp.int32)
    pick_match = (pick_table[:, :, None] == slots[None, None, :]).astype(jnp.float32)
    outputs = []
    grad_qnorms = []
    log_totals = []
    row_deltas = []
    band_parts = []
    partner_terms = []
    for head_index in range(HEADS):
        head_cols = slice(head_index * head_dim, (head_index + 1) * head_dim)
        head_queries = query_low[:, head_cols].reshape(blocks, BLOCK, head_dim)
        head_gradient = cotangent[:, head_cols].reshape(blocks, BLOCK, head_dim)
        head_keys = key_sets[0, ..., head_cols]
        head_values = key_sets[1, ..., head_cols]
        scores = (
            jnp.einsum(
                "gor,gxar->goxa", head_queries, head_keys, preferred_element_type=jnp.float32
            )
            * score_scale
        )
        row_total = jnp.sum(jnp.where(allowed, jnp.exp(scores), 0.0), axis=(2, 3))
        log_total = jnp.log(row_total)
        probability = jnp.where(allowed, jnp.exp(scores - log_total[:, :, None, None]), 0.0)
        attention_weight = probability.astype(jnp.bfloat16)
        output = jnp.einsum(
            "ieuz,iuzg->ieg", attention_weight, head_values, preferred_element_type=jnp.float32
        ).astype(jnp.bfloat16)
        row_delta = jnp.sum(head_gradient.astype(jnp.float32) * output.astype(jnp.float32), axis=-1)
        grad_prob = jnp.einsum(
            "gor,gxar->goxa", head_gradient, head_values, preferred_element_type=jnp.float32
        )
        score_gradient = (probability * (grad_prob - row_delta[:, :, None, None])).astype(
            jnp.bfloat16
        )
        grad_qnorm = (
            jnp.einsum(
                "ieuz,iuzg->ieg", score_gradient, head_keys, preferred_element_type=jnp.float32
            )
            * score_scale
        )
        key_terms = (
            jnp.einsum(
                "snwh,snc->swhc",
                score_gradient[:, :, :block_extent],
                head_queries,
                preferred_element_type=jnp.float32,
            )
            * score_scale
        )
        value_terms = jnp.einsum(
            "snwh,snc->swhc",
            attention_weight[:, :, :block_extent],
            head_gradient,
            preferred_element_type=jnp.float32,
        )
        band_buffer = jnp.zeros((2, blocks + 2 * BAND, BLOCK, head_dim), jnp.float32)
        for offset in range(block_extent):
            band_buffer = band_buffer.at[:, offset : offset + blocks].add(
                jnp.stack((key_terms[:, offset], value_terms[:, offset]))
            )
        far_keys = (
            jnp.einsum(
                "snwh,snc->swhc",
                score_gradient[:, :, block_extent:],
                head_queries,
                preferred_element_type=jnp.float32,
            )
            * score_scale
        )
        far_values = jnp.einsum(
            "snwh,snc->swhc",
            attention_weight[:, :, block_extent:],
            head_gradient,
            preferred_element_type=jnp.float32,
        )
        far_terms = jnp.stack((far_keys, far_values))
        partner_terms.append(
            jnp.einsum("ilb,gilkd->lgbkd", pick_match, far_terms, precision=lax.Precision.HIGHEST)
        )
        outputs.append(output)
        grad_qnorms.append(grad_qnorm)
        log_totals.append(log_total)
        row_deltas.append(row_delta)
        band_parts.append(band_buffer)
    band_all = jnp.concatenate(band_parts, axis=-1)
    local_grads = band_all[:, BAND : BAND + blocks]
    for shift_by in (1, -1):
        rim_part = band_all[:, BAND + blocks :] if shift_by == 1 else band_all[:, :BAND]
        arrived = from_behind(rim_part.astype(jnp.bfloat16), ("grp", "ctx"), shift_by).astype(
            rim_part.dtype
        )
        if shift_by == 1:
            local_grads = local_grads.at[:, :BAND].add(arrived)
        else:
            local_grads = local_grads.at[:, blocks - BAND :].add(arrived)
    partner_grads = jnp.concatenate(partner_terms, axis=-1)
    for level_index in level_order:
        bit_number = top_bit - 1 - level_index
        local_grads = local_grads + partner(
            partner_grads[level_index].astype(jnp.bfloat16), ("grp", "ctx"), bit_number
        ).astype(jnp.float32)
    output_all = jnp.concatenate(outputs, axis=-1).reshape(row_count, row_width)
    grad_qnorm_all = jnp.stack(grad_qnorms, axis=2).reshape(row_count, HEADS, head_dim)
    grad_query = (
        norm_back(grad_qnorm_all, q_normed, q_inverse, gain_query)
        .astype(jnp.bfloat16)
        .reshape(row_count, row_width)
    )
    grad_knorm = local_grads[0].reshape(row_count, HEADS, head_dim)
    grad_key = (
        norm_back(grad_knorm, k_normed, k_inverse, gain_key)
        .astype(jnp.bfloat16)
        .reshape(row_count, row_width)
    )
    grad_value = local_grads[1].astype(jnp.bfloat16).reshape(row_count, row_width)
    return (output_all, grad_query, grad_key, grad_value)


def solution(mesh):
    return jax.shard_map(
        body,
        mesh=mesh,
        in_specs=(
            P(("grp", "ctx"), None),
            P(("grp", "ctx"), None),
            P(("grp", "ctx"), None),
            P(("grp", "ctx")),
            P(("grp", "ctx"), None),
            P(),
            P(),
            P(("grp", "ctx"), None),
        ),
        out_specs=(
            P(("grp", "ctx"), None),
            P(("grp", "ctx"), None),
            P(("grp", "ctx"), None),
            P(("grp", "ctx"), None),
        ),
        check_vma=False,
    )
```

profile of v0, /device:TPU:4, one launch (start us, length us, event | category | flops | bytes accessed | tf_op | source)
XLA Modules:
  0.0 106.2 jit_solution(17674048999116945487)
XLA Ops:
  0.7 1.1 %reshape.599 = f32[256,2,128]{2,1,0:T(2,128)S(1)} reshape(bf16[256,256]{1,0:T(8,128)(2,1)} %param.39) | data formatting | bytes 393216 | tf_op jit(solution)/shard_map/reshape | solution.py:72
  3.6 0.7 pad_maximum_fusion.4
  4.4 5.8 %collective-permute-start.1 = (bf16[2,256,256]{2,1,0:T(8,128)(2,1)}, bf16[2,256,256]{2,1,0:T(8,128)(2,1)}, u32[]{:S(2)}, u32[]{:S(2)}) collective-permute-start(bf16[2,256,256]{2,1,0:T(8,128)(2,1)} %pad_maximum_fusion.4), channel_id=1, source_target_pairs={{1,0},{2,1},{3,2},{4,3},{5,4},{6,5},{7,6},{8,7},{9,8},{10,9},{11,1... | collective-permute-start | bytes 786440 | tf_op jit(solution)/shard_map/ppermute | solution.py:25
  10.2 1.9 %collective-permute-start = (bf16[2,256,256]{2,1,0:T(8,128)(2,1)}, bf16[2,256,256]{2,1,0:T(8,128)(2,1)}, u32[]{:S(2)}, u32[]{:S(2)}) collective-permute-start(bf16[2,256,256]{2,1,0:T(8,128)(2,1)} %pad_maximum_fusion.4), channel_id=1, source_target_pairs={{0,1},{1,2},{2,3},{3,4},{4,5},{5,6},{6,7},{7,8},{8,9},{9,10},{10,1... | collective-permute-start | bytes 786440 | tf_op jit(solution)/shard_map/ppermute | solution.py:23
  12.2 1.1 %collective-permute-start.3 = (bf16[2,256,256]{2,1,0:T(8,128)(2,1)}, bf16[2,256,256]{2,1,0:T(8,128)(2,1)S(1)}, u32[]{:S(2)}, u32[]{:S(2)}) collective-permute-start(bf16[2,256,256]{2,1,0:T(8,128)(2,1)} %pad_maximum_fusion.4), channel_id=1, source_target_pairs={{0,8},{1,9},{2,10},{3,11},{4,12},{5,13},{6,14},{7,15},{8,0},{9,1},... | collective-permute-start | bytes 786440 | tf_op jit(solution)/shard_map/ppermute | solution.py:35
  19.1 0.7 copy.260
  19.8 0.7 copy.258
  22.4 1.8 %collective-permute-start.5 = (bf16[2,256,256]{2,1,0:T(8,128)(2,1)}, bf16[2,256,256]{2,1,0:T(8,128)(2,1)}, u32[]{:S(2)}, u32[]{:S(2)}) collective-permute-start(bf16[2,256,256]{2,1,0:T(8,128)(2,1)} %pad_maximum_fusion.4), channel_id=1, source_target_pairs={{0,2},{1,3},{2,0},{3,1},{4,6},{5,7},{6,4},{7,5},{8,10},{9,11},{10,... | collective-permute-start | bytes 786440 | tf_op jit(solution)/shard_map/ppermute | solution.py:35
  24.3 1.1 %pad_maximum_fusion.3 = bf16[2,768,256]{2,1,0:T(8,128)(2,1)S(1)} fusion(bf16[2,256,256]{2,1,0:T(8,128)(2,1)} %collective-permute-done.1, bf16[1,256,256]{2,1,0:T(8,128)(2,1)S(1)} %bitcast.354, bf16[1,256,256]{2,1,0:T(8,128)(2,1)S(1)} %fusion.51, bf16[2,256,256]{2,1,0:T(8,128)(2,1)} %collective-permute-done), kind=kLoop, calls=%fused_computation.50 | loop fusion | flops 3145728 | bytes 1572864 | tf_op jit(solution)/shard_map/concatenate | solution.py:21
  26.1 0.7 fusion.48
  30.9 3.9 %collective-permute-done.5 = bf16[2,256,256]{2,1,0:T(8,128)(2,1)} collective-permute-done((bf16[2,256,256]{2,1,0:T(8,128)(2,1)}, bf16[2,256,256]{2,1,0:T(8,128)(2,1)}, u32[]{:S(2)}, u32[]{:S(2)}) %collective-permute-start.5) | collective-permute-done | bytes 262176 | tf_op jit(solution)/shard_map/ppermute | solution.py:35
  34.8 1.6 %gather_fusion.3 = bf16[2,2,128,256]{3,2,1,0:T(8,128)(2,1)S(1)} fusion(bf16[2,2,128,256]{3,2,1,0:T(8,128)(2,1)} %bitcast.26, s32[1024]{0:T(1024)} %pad_clamp_fusion), kind=kCustom, calls=%fused_computation.3.clone | custom fusion | bytes 524296 | tf_op jit(solution)/shard_map/jit(_take)/gather | solution.py:90
  36.4 0.8 bitcast_dynamic-update-slice_fusion.3
  37.3 0.9 bitcast_dynamic-update-slice_fusion.2
  38.1 0.8 bitcast_dynamic-update-slice_fusion.1
  38.9 0.8 bitcast_dynamic-update-slice_fusion
  39.8 1.4 %convolution_multiply_fusion = f32[2,128,9,128]{1,3,2,0:T(8,128)S(1)} fusion(bf16[2,128,128,1]{2,1,3,0:T(8,128)(2,1)S(1)} %bitcast.335, bf16[2,2,9,128,256]{4,3,2,1,0:T(8,128)(2,1)} %bitcast_dynamic-update-slice_fusion), kind=kOutput, calls=%fused_computation.15 | convolution fusion | flops 75792384 | bytes 1835008 | tf_op jit(solution)/shard_map/gor,gxar->goxa/dot_general | solution.py:119
  41.2 1.6 %select_reduce_fusion.1 = (f32[2,128]{1,0:T(2,128)S(1)}, f32[2,128]{1,0:T(2,128)S(1)}, f32[2,128,9,128]{1,3,2,0:T(8,128)S(1)}) fusion(pred[2,9]{1,0:T(4,128)(4,1)S(1)} %copy-done.54, f32[2,128,9,128]{1,3,2,0:T(8,128)S(1)} %convolution_multiply_fusion, bf16[2,128,128,1]{2,1,3,0:T(8,128)(2,1)S(1)} %bitcast.350, ...), kind=kOutput, calls=%fused_computation.30 | convolution fusion | flops 76971520 | bytes 3016722 | tf_op jit(solution)/shard_map/gor,gxar->goxa/dot_general | solution.py:119
  43.6 1.5 %multiply_reduce_fusion.7 = (f32[2,128]{1,0:T(2,128)S(1)}, bf16[2,128,128]{1,2,0:T(8,128)(2,1)S(1)}) fusion(bf16[2,128,128]{1,2,0:T(8,128)(2,1)S(1)} %copy-done.45, bf16[2,128,9,128]{1,3,2,0:T(8,128)(2,1)S(1)} %get-tuple-element.216, bf16[2,2,9,128,256]{4,3,2,1,0:T(8,128)(2,1)} %bitcast_dynamic-update-slice_fusion), kind=kOutput, calls=%fused_computation.158 | convolution fusion | flops 75661056 | bytes 1311744 | tf_op jit(solution)/shard_map/ieuz,iuzg->ieg/dot_general | solution.py:128
  45.1 1.4 %fusion.5 = bf16[2,128,9,128]{1,3,2,0:T(8,128)(2,1)S(1)} fusion(bf16[2,128,128,1]{2,1,3,0:T(8,128)(2,1)S(1)} %bitcast.343, f32[2,128,9,128]{1,3,2,0:T(8,128)S(1)} %get-tuple-element.218, f32[2,128]{1,0:T(2,128)S(1)} %get-tuple-element.221, f32[2,128]{1,0:T(2,128)S(1)} %log.14, pred[2,9]{1,0:T(4,128)(4,1)S(1)} %copy-done.54, ...), kind=kOutput, calls=%fused_computation.17 | convolution fusion | flops 76972032 | bytes 2426898 | tf_op jit(solution)/shard_map/gor,gxar->goxa/dot_general | solution.py:132
  46.5 2.1 %fusion.10 = f32[2,128,128]{2,1,0:T(8,128)} fusion(bf16[2,128,9,128]{1,3,2,0:T(8,128)(2,1)S(1)} %fusion.5, bf16[2,2,9,128,256]{4,3,2,1,0:T(8,128)(2,1)} %bitcast_dynamic-update-slice_fusion), kind=kOutput, calls=%fused_computation.34 | convolution fusion | flops 75530240 | bytes 1310720 | tf_op jit(solution)/shard_map/ieuz,iuzg->ieg/dot_general | solution.py:139
  49.0 1.5 %multiply_reduce_fusion.6 = (f32[2,128]{1,0:T(2,128)S(1)}, bf16[2,128,128]{1,2,0:T(8,128)(2,1)S(1)}) fusion(bf16[2,128,128]{1,2,0:T(8,128)(2,1)S(1)} %copy-done.44, bf16[2,128,9,128]{1,3,2,0:T(8,128)(2,1)S(1)} %get-tuple-element.217, bf16[2,2,9,128,256]{4,3,2,1,0:T(8,128)(2,1)} %bitcast_dynamic-update-slice_fusion), kind=kOutput, calls=%fused_computation.157 | convolution fusion | flops 75661056 | bytes 1311744 | tf_op jit(solution)/shard_map/ieuz,iuzg->ieg/dot_general | solution.py:128
  50.4 1.0 convolution_bitcast_fusion
  51.5 1.5 %fusion.6 = bf16[2,128,9,128]{1,3,2,0:T(8,128)(2,1)S(1)} fusion(bf16[2,128,128,1]{2,1,3,0:T(8,128)(2,1)S(1)} %bitcast.340, f32[2,128,9,128]{1,3,2,0:T(8,128)S(1)} %convolution_multiply_fusion, f32[2,128]{1,0:T(2,128)S(1)} %get-tuple-element.219, f32[2,128]{1,0:T(2,128)S(1)} %log.15, pred[2,9]{1,0:T(4,128)(4,1)S(1)} %copy-done.54, ...), kind=kOutput, calls=%fused_computation.18 | convolution fusion | flops 76972032 | bytes 2426898 | tf_op jit(solution)/shard_map/gor,gxar->goxa/dot_general | solution.py:132
  52.9 2.1 %fusion.9 = f32[2,128,128]{2,1,0:T(8,128)} fusion(bf16[2,128,9,128]{1,3,2,0:T(8,128)(2,1)S(1)} %fusion.6, bf16[2,2,9,128,256]{4,3,2,1,0:T(8,128)(2,1)} %bitcast_dynamic-update-slice_fusion), kind=kOutput, calls=%fused_computation.32 | convolution fusion | flops 75530240 | bytes 1310720 | tf_op jit(solution)/shard_map/ieuz,iuzg->ieg/dot_general | solution.py:139
  55.1 1.0 fusion.7
  56.1 1.0 convolution_bitcast_fusion.1
  57.1 1.0 fusion.8
  58.8 1.7 %copy.257 = bf16[2,128,256]{2,1,0:T(8,128)(2,1)} copy(bf16[2,128,256]{1,2,0:T(8,128)(2,1)} %pad_maximum_fusion.6) | data formatting | bytes 262144 | tf_op jit(solution)/shard_map/concatenate | solution.py:205
  60.4 2.5 %multiply_reduce_fusion.4 = (f32[256,2]{0,1:T(2,128)}, f32[256,2]{0,1:T(2,128)S(1)}, f32[2,32,8,128]{3,2,1,0:T(8,128)}) fusion(f32[256,1,128]{2,0,1:T(8,128)} %bitcast.356, f32[256,1,128]{2,0,1:T(8,128)} %bitcast.355, f32[2,128]{1,0:T(2,128)S(1)} %copy-done.47, f32[256,2]{0,1:T(2,128)S(1)} %add_rsqrt_fusion.1, f32[256,2]{0,1:T(2,128)S(1)} %broadcast_multiply_fusion.5, ...), kind=kLoop, calls=%fused_computation.131 | loop fusion | flops 523264 | bytes 664576 | tf_op jit(solution)/shard_map/reduce_sum | solution.py:54
  62.9 0.8 copy.264
  64.4 0.8 copy.263
  65.5 0.8 slice_bitcast_fusion.31
  66.3 0.9 slice_bitcast_fusion.32
  67.5 0.8 slice_bitcast_fusion.21
  68.6 0.8 slice_bitcast_fusion.22
  69.5 2.6 %fusion.13 = bf16[4,2,128,128,2]{3,4,2,1,0:T(2,128)(2,1)S(1)} fusion(f32[2,2,4,128,128]{4,3,2,1,0:T(8,128)S(1)} %pad_maximum_fusion.2, s32[2,4]{0,1:T(4,128)S(1)} %copy-done.49), kind=kOutput, calls=%fused_computation.41 | convolution fusion | flops 6291472 | bytes 1572896 | tf_op jit(solution)/shard_map/ilb,gilkd->lgbkd/dot_general | solution.py:181
  72.8 2.6 %fusion.15 = bf16[4,2,128,128,2]{3,4,2,1,0:T(2,128)(2,1)S(1)} fusion(f32[2,2,4,128,128]{4,3,2,1,0:T(8,128)S(1)} %pad_maximum_fusion.1, s32[2,4]{0,1:T(4,128)S(1)} %copy-done.49), kind=kOutput, calls=%fused_computation.43 | convolution fusion | flops 6291472 | bytes 1572896 | tf_op jit(solution)/shard_map/ilb,gilkd->lgbkd/dot_general | solution.py:181
  76.2 3.1 %collective-permute-start.10 = (bf16[2,2,128,256]{2,3,1,0:T(8,128)(2,1)S(1)}, bf16[2,2,128,256]{2,3,1,0:T(8,128)(2,1)S(1)}, u32[]{:S(2)}, u32[]{:S(2)}) collective-permute-start(bf16[2,2,128,256]{2,3,1,0:T(8,128)(2,1)S(1)} %get-tuple-element.181), channel_id=1, source_target_pairs={{0,4},{1,5},{2,6},{3,7},{4,0},{5,1},{6,2},{7,3},{8,12},{9,13},{10,... | collective-permute-start | bytes 786440 | tf_op jit(solution)/shard_map/ppermute | solution.py:35
  79.3 1.5 %collective-permute-start.9 = (bf16[2,2,128,256]{2,3,1,0:T(8,128)(2,1)S(1)}, bf16[2,2,128,256]{2,3,1,0:T(8,128)(2,1)S(1)}, u32[]{:S(2)}, u32[]{:S(2)}) collective-permute-start(bf16[2,2,128,256]{2,3,1,0:T(8,128)(2,1)S(1)} %get-tuple-element.182), channel_id=1, source_target_pairs={{0,8},{1,9},{2,10},{3,11},{4,12},{5,13},{6,14},{7,15},{8,0},{9,1},... | collective-permute-start | bytes 786440 | tf_op jit(solution)/shard_map/ppermute | solution.py:35
  83.7 2.8 %collective-permute-start.7 = (bf16[2,2,128,256]{2,3,1,0:T(8,128)(2,1)S(1)}, bf16[2,2,128,256]{2,3,1,0:T(8,128)(2,1)S(1)}, u32[]{:S(2)}, u32[]{:S(2)}) collective-permute-start(bf16[2,2,128,256]{2,3,1,0:T(8,128)(2,1)S(1)} %get-tuple-element.184), channel_id=1, source_target_pairs={{1,0},{2,1},{3,2},{4,3},{5,4},{6,5},{7,6},{8,7},{9,8},{10,9},{11,1... | collective-permute-start | bytes 786440 | tf_op jit(solution)/shard_map/ppermute | solution.py:41
  86.5 3.4 %collective-permute-done.11 = bf16[2,2,128,256]{2,3,1,0:T(8,128)(2,1)S(1)} collective-permute-done((bf16[2,2,128,256]{2,3,1,0:T(8,128)(2,1)S(1)}, bf16[2,2,128,256]{2,3,1,0:T(8,128)(2,1)S(1)}, u32[]{:S(2)}, u32[]{:S(2)}) %collective-permute-start.11) | collective-permute-done | bytes 262176 | tf_op jit(solution)/shard_map/ppermute | solution.py:35
  89.9 1.9 %collective-permute-start.6 = (bf16[2,2,128,256]{2,3,1,0:T(8,128)(2,1)S(1)}, bf16[2,2,128,256]{2,3,1,0:T(8,128)(2,1)S(1)}, u32[]{:S(2)}, u32[]{:S(2)}) collective-permute-start(bf16[2,2,128,256]{2,3,1,0:T(8,128)(2,1)S(1)} %get-tuple-element.183), channel_id=1, source_target_pairs={{0,1},{1,2},{2,3},{3,4},{4,5},{5,6},{6,7},{7,8},{8,9},{9,10},{10,1... | collective-permute-start | bytes 786440 | tf_op jit(solution)/shard_map/ppermute | solution.py:41
  92.5 0.7 fusion.36
  93.3 7.9 %collective-permute-done.6 = bf16[2,2,128,256]{2,3,1,0:T(8,128)(2,1)S(1)} collective-permute-done((bf16[2,2,128,256]{2,3,1,0:T(8,128)(2,1)S(1)}, bf16[2,2,128,256]{2,3,1,0:T(8,128)(2,1)S(1)}, u32[]{:S(2)}, u32[]{:S(2)}) %collective-permute-start.6) | collective-permute-done | bytes 262176 | tf_op jit(solution)/shard_map/ppermute | solution.py:41
  102.4 1.6 %multiply_reduce_fusion.5 = (f32[256,2]{1,0:T(8,128)S(1)}, f32[256,2]{1,0:T(8,128)S(1)}) fusion(f32[256,2,128]{2,1,0:T(2,128)S(1)} %reshape_squeeze.6, f32[2,128]{1,0:T(2,128)S(1)} %copy-done.48, f32[256,2]{1,0:T(8,128)S(1)} %copy-done.12, f32[256,2,128]{2,1,0:T(2,128)S(1)} %reshape.599, f32[256,2]{1,0:T(8,128)S(1)} %copy-done.6), kind=kLoop, calls=%fused_computation.132 | loop fusion | flops 392192 | bytes 533504 | tf_op jit(solution)/shard_map/reduce_sum | solution.py:54
  104.0 0.8 copy.300
  105.5 0.8 fusion.33
  (210 shorter events, 24.2 us)
Async XLA Ops:
  2.1 11.3 %copy-start = (bf16[256,256]{1,0:T(8,128)(2,1)S(1)}, bf16[256,256]{1,0:T(8,128)(2,1)}, u32[]{:S(2)}) copy-start(bf16[256,256]{1,0:T(8,128)(2,1)} %param.38) | copy-start | bytes 393220
  2.1 11.4 %copy-start.5 = (f32[256,2]{1,0:T(8,128)}, f32[256,2]{1,0:T(8,128)S(1)}, u32[]{:S(2)}) copy-start(f32[256,2]{1,0:T(8,128)S(1)} %broadcast_multiply_fusion.2) | copy-start | bytes 6148
  2.8 11.4 %copy-start.11 = (f32[256,2]{1,0:T(8,128)}, f32[256,2]{1,0:T(8,128)S(1)}, u32[]{:S(2)}) copy-start(f32[256,2]{1,0:T(8,128)S(1)} %add_rsqrt_fusion) | copy-start | bytes 6148
  2.8 11.5 %copy-start.46 = (s32[2,4]{1,0:T(2,128)S(1)}, s32[2,4]{1,0:T(2,128)}, u32[]{:S(2)}) copy-start(s32[2,4]{1,0:T(2,128)} %param.42) | copy-start | bytes 100
  3.2 13.5 %copy-start.43 = (bf16[256,256]{1,0:T(8,128)(2,1)S(1)}, bf16[256,256]{1,0:T(8,128)(2,1)}, u32[]{:S(2)}) copy-start(bf16[256,256]{1,0:T(8,128)(2,1)} %param.45) | copy-start | bytes 393220
  3.6 15.2 %copy-start.47 = (f32[2,128]{1,0:T(2,128)S(1)}, f32[2,128]{1,0:T(2,128)}, u32[]{:S(2)}) copy-start(f32[2,128]{1,0:T(2,128)} %param.43) | copy-start | bytes 3076
  4.4 18.1 %collective-permute-start.1 = (bf16[2,256,256]{2,1,0:T(8,128)(2,1)}, bf16[2,256,256]{2,1,0:T(8,128)(2,1)}, u32[]{:S(2)}, u32[]{:S(2)}) collective-permute-start(bf16[2,256,256]{2,1,0:T(8,128)(2,1)} %pad_maximum_fusion.4), channel_id=1, source_target_pairs={{1,0},{2,1},{3,2},{4,3},{5,4},{6,5},{7,6},{8,7},{9,8},{10,9},{11,1... | collective-permute-start | bytes 786440 | tf_op jit(solution)/shard_map/ppermute | solution.py:25
  10.2 14.1 %collective-permute-start = (bf16[2,256,256]{2,1,0:T(8,128)(2,1)}, bf16[2,256,256]{2,1,0:T(8,128)(2,1)}, u32[]{:S(2)}, u32[]{:S(2)}) collective-permute-start(bf16[2,256,256]{2,1,0:T(8,128)(2,1)} %pad_maximum_fusion.4), channel_id=1, source_target_pairs={{0,1},{1,2},{2,3},{3,4},{4,5},{5,6},{6,7},{7,8},{8,9},{9,10},{10,1... | collective-permute-start | bytes 786440 | tf_op jit(solution)/shard_map/ppermute | solution.py:23
  12.1 16.2 %collective-permute-start.2 = (bf16[2,256,256]{2,1,0:T(8,128)(2,1)}, bf16[2,256,256]{2,1,0:T(8,128)(2,1)S(1)}, u32[]{:S(2)}, u32[]{:S(2)}) collective-permute-start(bf16[2,256,256]{2,1,0:T(8,128)(2,1)} %pad_maximum_fusion.4), channel_id=1, source_target_pairs={{0,16},{1,17},{2,18},{3,19},{4,20},{5,21},{6,22},{7,23},{8,24},{9,... | collective-permute-start | bytes 786440 | tf_op jit(solution)/shard_map/ppermute | solution.py:35
  12.2 16.7 %collective-permute-start.3 = (bf16[2,256,256]{2,1,0:T(8,128)(2,1)}, bf16[2,256,256]{2,1,0:T(8,128)(2,1)S(1)}, u32[]{:S(2)}, u32[]{:S(2)}) collective-permute-start(bf16[2,256,256]{2,1,0:T(8,128)(2,1)} %pad_maximum_fusion.4), channel_id=1, source_target_pairs={{0,8},{1,9},{2,10},{3,11},{4,12},{5,13},{6,14},{7,15},{8,0},{9,1},... | collective-permute-start | bytes 786440 | tf_op jit(solution)/shard_map/ppermute | solution.py:35
  13.3 16.2 %collective-permute-start.4 = (bf16[2,256,256]{2,1,0:T(8,128)(2,1)}, bf16[2,256,256]{2,1,0:T(8,128)(2,1)S(1)}, u32[]{:S(2)}, u32[]{:S(2)}) collective-permute-start(bf16[2,256,256]{2,1,0:T(8,128)(2,1)} %pad_maximum_fusion.4), channel_id=1, source_target_pairs={{0,4},{1,5},{2,6},{3,7},{4,0},{5,1},{6,2},{7,3},{8,12},{9,13},{10,... | collective-permute-start | bytes 786440 | tf_op jit(solution)/shard_map/ppermute | solution.py:35
  13.4 5.5 %copy-start.55 = (s32[2]{0:T(128)S(1)}, s32[2]{0:T(128)}, u32[]{:S(2)}) copy-start(s32[2]{0:T(128)} %param.41) | copy-start | bytes 28
  16.7 7.6 %copy-start.17 = (bf16[256,128]{1,0:T(8,128)(2,1)}, bf16[256,128]{1,0:T(8,128)(2,1)S(1)}, u32[]{:S(2)}) copy-start(bf16[256,128]{1,0:T(8,128)(2,1)S(1)} %get-tuple-element.207) | copy-start | bytes 196612
  16.7 28.3 %copy-start.19 = (bf16[256,128]{1,0:T(8,128)(2,1)}, bf16[256,128]{1,0:T(8,128)(2,1)S(1)}, u32[]{:S(2)}) copy-start(bf16[256,128]{1,0:T(8,128)(2,1)S(1)} %get-tuple-element.206) | copy-start | bytes 196612
  18.5 6.9 %copy-start.1 = (f32[256,2,128]{2,1,0:T(2,128)}, f32[256,2,128]{2,1,0:T(2,128)S(1)}, u32[]{:S(2)}) copy-start(f32[256,2,128]{2,1,0:T(2,128)S(1)} %mul.195.clone) | copy-start | bytes 786436
  18.8 7.3 %copy-start.3 = (f32[256,2,128]{2,1,0:T(2,128)}, f32[256,2,128]{2,1,0:T(2,128)S(1)}, u32[]{:S(2)}) copy-start(f32[256,2,128]{2,1,0:T(2,128)S(1)} %sub.147.clone) | copy-start | bytes 786436
  22.4 17.3 %copy-start.15 = (bf16[256,128]{1,0:T(8,128)(2,1)}, bf16[256,128]{1,0:T(8,128)(2,1)S(1)}, u32[]{:S(2)}) copy-start(bf16[256,128]{1,0:T(8,128)(2,1)S(1)} %get-tuple-element.209) | copy-start | bytes 196612
  22.4 12.3 %collective-permute-start.5 = (bf16[2,256,256]{2,1,0:T(8,128)(2,1)}, bf16[2,256,256]{2,1,0:T(8,128)(2,1)}, u32[]{:S(2)}, u32[]{:S(2)}) collective-permute-start(bf16[2,256,256]{2,1,0:T(8,128)(2,1)} %pad_maximum_fusion.4), channel_id=1, source_target_pairs={{0,2},{1,3},{2,0},{3,1},{4,6},{5,7},{6,4},{7,5},{8,10},{9,11},{10,... | collective-permute-start | bytes 786440 | tf_op jit(solution)/shard_map/ppermute | solution.py:35
  27.6 8.9 %copy-start.53 = (pred[2]{0:T(512)(128)(4,1)S(1)}, pred[2]{0:T(512)(128)(4,1)}, u32[]{:S(2)}) copy-start(pred[2]{0:T(512)(128)(4,1)} %compare_and_fusion.3) | copy-start | bytes 10
  28.3 9.0 %copy-start.52 = (pred[2]{0:T(512)(128)(4,1)S(1)}, pred[2]{0:T(512)(128)(4,1)}, u32[]{:S(2)}) copy-start(pred[2]{0:T(512)(128)(4,1)} %compare_and_fusion.2) | copy-start | bytes 10
  28.9 9.2 %copy-start.51 = (pred[2]{0:T(512)(128)(4,1)S(1)}, pred[2]{0:T(512)(128)(4,1)}, u32[]{:S(2)}) copy-start(pred[2]{0:T(512)(128)(4,1)} %compare_and_fusion.1) | copy-start | bytes 10
  29.5 9.5 %copy-start.50 = (pred[2]{0:T(512)(128)(4,1)S(1)}, pred[2]{0:T(512)(128)(4,1)}, u32[]{:S(2)}) copy-start(pred[2]{0:T(512)(128)(4,1)} %compare_and_fusion) | copy-start | bytes 10
  38.1 3.0 %copy-start.22 = (bf16[256,128]{1,0:T(8,128)(2,1)S(1)}, bf16[256,128]{1,0:T(8,128)(2,1)}, u32[]{:S(2)}) copy-start(bf16[256,128]{1,0:T(8,128)(2,1)} %get-tuple-element.208) | copy-start | bytes 196612
  38.1 3.0 %copy-start.54 = (pred[2,9]{1,0:T(4,128)(4,1)S(1)}, pred[2,9]{1,0:T(4,128)(4,1)}, u32[]{:S(2)}) copy-start(pred[2,9]{1,0:T(4,128)(4,1)} %concatenate.43) | copy-start | bytes 58
  51.4 3.6 %copy-start.16 = (bf16[256,128]{1,0:T(8,128)(2,1)S(1)}, bf16[256,128]{1,0:T(8,128)(2,1)}, u32[]{:S(2)}) copy-start(bf16[256,128]{1,0:T(8,128)(2,1)} %copy-done.15) | copy-start | bytes 196612
  52.9 3.2 %copy-start.20 = (bf16[256,128]{1,0:T(8,128)(2,1)S(1)}, bf16[256,128]{1,0:T(8,128)(2,1)}, u32[]{:S(2)}) copy-start(bf16[256,128]{1,0:T(8,128)(2,1)} %copy-done.19) | copy-start | bytes 196612
  69.5 3.2 %copy-start.8 = (f32[1,2,4,128,128]{4,3,2,1,0:T(8,128)S(1)}, f32[1,2,4,128,128]{4,3,2,1,0:T(8,128)}, u32[]{:S(2)}) copy-start(f32[1,2,4,128,128]{4,3,2,1,0:T(8,128)} %convolution_bitcast_fusion.1) | copy-start | bytes 1572868
  69.5 3.2 %copy-start.9 = (f32[1,2,4,128,128]{4,3,2,1,0:T(8,128)S(1)}, f32[1,2,4,128,128]{4,3,2,1,0:T(8,128)}, u32[]{:S(2)}) copy-start(f32[1,2,4,128,128]{4,3,2,1,0:T(8,128)} %fusion.8) | copy-start | bytes 1572868
  76.0 5.4 %copy-start.39 = (f32[1,2,128,128]{2,3,1,0:T(8,128)S(1)}, f32[1,2,128,128]{2,3,1,0:T(8,128)}, u32[]{:S(2)}) copy-start(f32[1,2,128,128]{2,3,1,0:T(8,128)} %get-tuple-element.204) | copy-start | bytes 393220
  76.0 5.4 %copy-start.40 = (f32[1,2,128,128]{2,3,1,0:T(8,128)S(1)}, f32[1,2,128,128]{2,3,1,0:T(8,128)}, u32[]{:S(2)}) copy-start(f32[1,2,128,128]{2,3,1,0:T(8,128)} %get-tuple-element.198) | copy-start | bytes 393220
  76.0 5.5 %copy-start.41 = (f32[1,2,128,128]{2,3,1,0:T(8,128)S(1)}, f32[1,2,128,128]{2,3,1,0:T(8,128)}, u32[]{:S(2)}) copy-start(f32[1,2,128,128]{2,3,1,0:T(8,128)} %get-tuple-element.194) | copy-start | bytes 393220
  76.0 5.5 %copy-start.42 = (f32[1,2,128,128]{2,3,1,0:T(8,128)S(1)}, f32[1,2,128,128]{2,3,1,0:T(8,128)}, u32[]{:S(2)}) copy-start(f32[1,2,128,128]{2,3,1,0:T(8,128)} %get-tuple-element.189) | copy-start | bytes 393220
  76.1 5.5 %copy-start.32 = (f32[1,2,128,128]{2,3,1,0:T(8,128)S(1)}, f32[1,2,128,128]{2,3,1,0:T(8,128)}, u32[]{:S(2)}) copy-start(f32[1,2,128,128]{2,3,1,0:T(8,128)} %get-tuple-element.203) | copy-start | bytes 393220
  76.1 5.5 %copy-start.37 = (f32[1,2,128,128]{2,3,1,0:T(8,128)S(1)}, f32[1,2,128,128]{2,3,1,0:T(8,128)}, u32[]{:S(2)}) copy-start(f32[1,2,128,128]{2,3,1,0:T(8,128)} %get-tuple-element.197) | copy-start | bytes 393220
  76.1 5.6 %copy-start.30 = (f32[1,2,128,128]{2,3,1,0:T(8,128)S(1)}, f32[1,2,128,128]{2,3,1,0:T(8,128)}, u32[]{:S(2)}) copy-start(f32[1,2,128,128]{2,3,1,0:T(8,128)} %get-tuple-element.202) | copy-start | bytes 393220
  76.1 5.6 %copy-start.35 = (f32[1,2,128,128]{2,3,1,0:T(8,128)S(1)}, f32[1,2,128,128]{2,3,1,0:T(8,128)}, u32[]{:S(2)}) copy-start(f32[1,2,128,128]{2,3,1,0:T(8,128)} %get-tuple-element.196) | copy-start | bytes 393220
  76.1 13.8 %collective-permute-start.11 = (bf16[2,2,128,256]{2,3,1,0:T(8,128)(2,1)S(1)}, bf16[2,2,128,256]{2,3,1,0:T(8,128)(2,1)S(1)}, u32[]{:S(2)}, u32[]{:S(2)}) collective-permute-start(bf16[2,2,128,256]{2,3,1,0:T(8,128)(2,1)S(1)} %get-tuple-element.180), channel_id=1, source_target_pairs={{0,2},{1,3},{2,0},{3,1},{4,6},{5,7},{6,4},{7,5},{8,10},{9,11},{10,... | collective-permute-start | bytes 786440 | tf_op jit(solution)/shard_map/ppermute | solution.py:35
  76.2 17.1 %collective-permute-start.10 = (bf16[2,2,128,256]{2,3,1,0:T(8,128)(2,1)S(1)}, bf16[2,2,128,256]{2,3,1,0:T(8,128)(2,1)S(1)}, u32[]{:S(2)}, u32[]{:S(2)}) collective-permute-start(bf16[2,2,128,256]{2,3,1,0:T(8,128)(2,1)S(1)} %get-tuple-element.181), channel_id=1, source_target_pairs={{0,4},{1,5},{2,6},{3,7},{4,0},{5,1},{6,2},{7,3},{8,12},{9,13},{10,... | collective-permute-start | bytes 786440 | tf_op jit(solution)/shard_map/ppermute | solution.py:35
  79.3 14.0 %collective-permute-start.9 = (bf16[2,2,128,256]{2,3,1,0:T(8,128)(2,1)S(1)}, bf16[2,2,128,256]{2,3,1,0:T(8,128)(2,1)S(1)}, u32[]{:S(2)}, u32[]{:S(2)}) collective-permute-start(bf16[2,2,128,256]{2,3,1,0:T(8,128)(2,1)S(1)} %get-tuple-element.182), channel_id=1, source_target_pairs={{0,8},{1,9},{2,10},{3,11},{4,12},{5,13},{6,14},{7,15},{8,0},{9,1},... | collective-permute-start | bytes 786440 | tf_op jit(solution)/shard_map/ppermute | solution.py:35
  80.8 12.5 %collective-permute-start.8 = (bf16[2,2,128,256]{2,3,1,0:T(8,128)(2,1)S(1)}, bf16[2,2,128,256]{2,3,1,0:T(8,128)(2,1)S(1)}, u32[]{:S(2)}, u32[]{:S(2)}) collective-permute-start(bf16[2,2,128,256]{2,3,1,0:T(8,128)(2,1)S(1)} %get-tuple-element.179), channel_id=1, source_target_pairs={{0,16},{1,17},{2,18},{3,19},{4,20},{5,21},{6,22},{7,23},{8,24},{9,... | collective-permute-start | bytes 786440 | tf_op jit(solution)/shard_map/ppermute | solution.py:35
  83.5 8.3 %copy-start.23 = (f32[256,2]{1,0:T(8,128)S(1)}, f32[256,2]{1,0:T(8,128)}, u32[]{:S(2)}) copy-start(f32[256,2]{1,0:T(8,128)} %copy.264) | copy-start | bytes 6148
  83.5 8.6 %copy-start.24 = (f32[256,2]{1,0:T(8,128)S(1)}, f32[256,2]{1,0:T(8,128)}, u32[]{:S(2)}) copy-start(f32[256,2]{1,0:T(8,128)} %copy.263) | copy-start | bytes 6148
  83.5 9.0 %copy-start.2 = (f32[256,2,128]{2,1,0:T(2,128)S(1)}, f32[256,2,128]{2,1,0:T(2,128)}, u32[]{:S(2)}) copy-start(f32[256,2,128]{2,1,0:T(2,128)} %copy-done.1) | copy-start | bytes 786436
  83.6 9.0 %copy-start.4 = (f32[256,2,128]{2,1,0:T(2,128)S(1)}, f32[256,2,128]{2,1,0:T(2,128)}, u32[]{:S(2)}) copy-start(f32[256,2,128]{2,1,0:T(2,128)} %copy-done.3) | copy-start | bytes 786436
  83.6 9.0 %copy-start.21 = (f32[2,32,8,128]{3,2,1,0:T(8,128)S(1)}, f32[2,32,8,128]{3,2,1,0:T(8,128)}, u32[]{:S(2)}) copy-start(f32[2,32,8,128]{3,2,1,0:T(8,128)} %get-tuple-element.205) | copy-start | bytes 786436
  83.7 9.6 %collective-permute-start.7 = (bf16[2,2,128,256]{2,3,1,0:T(8,128)(2,1)S(1)}, bf16[2,2,128,256]{2,3,1,0:T(8,128)(2,1)S(1)}, u32[]{:S(2)}, u32[]{:S(2)}) collective-permute-start(bf16[2,2,128,256]{2,3,1,0:T(8,128)(2,1)S(1)} %get-tuple-element.184), channel_id=1, source_target_pairs={{1,0},{2,1},{3,2},{4,3},{5,4},{6,5},{7,6},{8,7},{9,8},{10,9},{11,1... | collective-permute-start | bytes 786440 | tf_op jit(solution)/shard_map/ppermute | solution.py:41
  89.9 11.3 %collective-permute-start.6 = (bf16[2,2,128,256]{2,3,1,0:T(8,128)(2,1)S(1)}, bf16[2,2,128,256]{2,3,1,0:T(8,128)(2,1)S(1)}, u32[]{:S(2)}, u32[]{:S(2)}) collective-permute-start(bf16[2,2,128,256]{2,3,1,0:T(8,128)(2,1)S(1)} %get-tuple-element.183), channel_id=1, source_target_pairs={{0,1},{1,2},{2,3},{3,4},{4,5},{5,6},{6,7},{7,8},{8,9},{9,10},{10,1... | collective-permute-start | bytes 786440 | tf_op jit(solution)/shard_map/ppermute | solution.py:41
  101.6 3.8 %copy-start.14 = (bf16[256,256]{1,0:T(8,128)(2,1)S(1)}, bf16[256,256]{1,0:T(8,128)(2,1)}, u32[]{:S(2)}) copy-start(bf16[256,256]{1,0:T(8,128)(2,1)} %param.39) | copy-start | bytes 393220
  (20 other events, 28.5 us)
where the time goes:
time: 107 us; the launch traced here: 106 us
  local copies, waits for them, and re-layouts  26.1 us (24%)
  matrix products  23.4 us (22%)
  starting transfers between devices  20.7 us (19%)
  other arithmetic  19 us (18%)
  waiting for transfers between devices  15.2 us (14%)
  between operations  1.79 us (2%)
    ppermute x8, starting transfers between devices, partner(): return lax.ppermute(value, axis, pairs)  8.32 us
    ppermute x2, waiting for transfers between devices, from_behind(): return lax.ppermute(x, axis, pairs)  7.88 us
    ppermute x8, waiting for transfers between devices, partner(): return lax.ppermute(value, axis, pairs)  7.29 us
    unnamed x119, local copies, waits for them, and re-layouts  6.49 us
    ppermute x1, starting transfers between devices, with_halo(): lax.ppermute(head, axis, [((i + 1) % count, i) for i in range(ends)])  5.81 us
    dot_general x2, matrix products, body(): jnp.einsum('ilb,gilkd->lgbkd', pick_match, far_terms, precision=lax.Preci...  5.14 us
    ppermute x2, starting transfers between devices, from_behind(): return lax.ppermute(x, axis, pairs)  4.66 us
    dot_general x2, matrix products, body(): jnp.einsum('ieuz,iuzg->ieg', score_gradient, head_keys, preferred_element...  4.27 us
  transfers between devices with their start and end apart: 12, of which 3 were waited for; matrix products, arithmetic and copies ran while one was open for 17% of the time, Pallas kernels for 0%

commit v1 on v0

v1 whole, which is shorter than its diff:
```python
import functools
import math

import jax
import jax.numpy as jnp
from jax import lax
from jax.experimental import pallas as pl
from jax.experimental.pallas import tpu as pltpu
from jax.sharding import PartitionSpec as P

HEADS = 2
BLOCK = 128
LEVELS = 4
BAND = 2
EPS = 1e-05
AXES = ("grp", "ctx")
MESH = pl.DeviceIdType.MESH
F32 = jnp.float32
BF16 = jnp.bfloat16
LEFT, RIGHT = 0, 1
SLOTS = 2 + LEVELS
KEY, VAL, QRY, COT, STAT = 0, 1, 2, 3, 4
POS = 2 * BAND + 1 + LEVELS


def dot_t(a, b):
    return lax.dot_general(a, b, (((1,), (1,)), ((), ())), preferred_element_type=F32)


def dot_n(a, b):
    return jnp.dot(a, b, preferred_element_type=F32)


def rows(block):
    return pl.ds(block * BLOCK, BLOCK)


def kernel(
    shards,
    inner,
    q_ref,
    k_ref,
    v_ref,
    g_ref,
    gq_ref,
    gk_ref,
    reach_ref,
    part_ref,
    o_ref,
    dq_ref,
    dk_ref,
    dv_ref,
    buf,
    stat,
    own_stat,
    out_stat,
    qn,
    kn,
    qhat,
    khat,
    qinv,
    kinv,
    kcat,
    vcat,
    e_s,
    g_s,
    dk_acc,
    dv_acc,
    send_sem,
    recv_sem,
    fwd_sem,
):
    me = lax.axis_index(AXES)
    hd = gq_ref.shape[1]
    scale = hd ** (-0.5)
    log2e_scale = scale * math.log2(math.e)
    masks = [shards >> (level + 1) for level in range(LEVELS)]
    relay = 2 in masks
    near = 2 + masks.index(2) if relay else None
    has_left = me > 0
    has_right = me < shards - 1
    core = lax.rem(me, 2)
    chip_odd = lax.rem(me // 2, 2)
    peers = [jnp.bitwise_xor(me, m) for m in masks]

    def at(t):
        return (t // inner, lax.rem(t, inner))

    barrier = pltpu.get_barrier_semaphore()
    for t in peers:
        pl.semaphore_signal(barrier, inc=1, device_id=at(t), device_id_type=MESH)

    @pl.when(has_left)
    def _():
        pl.semaphore_signal(barrier, inc=1, device_id=at(me - 1), device_id_type=MESH)

    @pl.when(has_right)
    def _():
        pl.semaphore_signal(barrier, inc=1, device_id=at(me + 1), device_id_type=MESH)

    pl.semaphore_wait(
        barrier, LEVELS + has_left.astype(jnp.int32) + has_right.astype(jnp.int32)
    )

    sources = {KEY: kn, VAL: v_ref, QRY: qn, COT: g_ref}

    def copy(slot, what, t):
        if what == STAT:
            src, dst = out_stat.at[slot], stat.at[slot]
        else:
            src, dst = sources[what], buf.at[slot, what]
        return pltpu.make_async_remote_copy(
            src_ref=src,
            dst_ref=dst,
            send_sem=send_sem.at[slot, what],
            recv_sem=recv_sem.at[slot, what],
            device_id=at(t),
            device_id_type=MESH,
        )

    def forward(slot, what, t):
        return pltpu.make_async_remote_copy(
            src_ref=buf.at[near, what],
            dst_ref=buf.at[slot, what],
            send_sem=fwd_sem.at[what],
            recv_sem=recv_sem.at[slot, what],
            device_id=at(t),
            device_id_type=MESH,
        )

    def to_right(what):
        if relay and what != STAT:
            return has_right & ((core == 0) | (chip_odd == 1))
        return has_right

    def to_left(what):
        if relay and what != STAT:
            return has_left & ((core == 1) | (chip_odd == 0))
        return has_left

    def each_copy(what, act):
        for level in reversed(range(LEVELS)):
            act(copy(2 + level, what, peers[level]))

        @pl.when(to_right(what))
        def _():
            act(copy(LEFT, what, me + 1))

        @pl.when(to_left(what))
        def _():
            act(copy(RIGHT, what, me - 1))

    def send(what):
        each_copy(what, lambda c: c.start())

    def arrived(slot, what):
        if slot == LEFT:

            @pl.when(has_left)
            def _():
                copy(LEFT, what, me - 1).wait_recv()
        elif slot == RIGHT:

            @pl.when(has_right)
            def _():
                copy(RIGHT, what, me + 1).wait_recv()
        else:
            copy(slot, what, peers[slot - 2]).wait_recv()

    def each_forward(what, act):
        if not relay:
            return

        @pl.when((core == 0) & (chip_odd == 0))
        def _():
            act(forward(RIGHT, what, me + 1))

        @pl.when((core == 1) & (chip_odd == 1))
        def _():
            act(forward(LEFT, what, me - 1))

    send(VAL)

    def normalize(x_ref, gain_ref, hat_ref, inv_ref, out_ref):
        for h in range(HEADS):
            cols = slice(h * hd, (h + 1) * hd)
            x = x_ref[:, cols].astype(F32)
            x = x - jnp.mean(x, axis=-1, keepdims=True)
            inv = lax.rsqrt(jnp.mean(x * x, axis=-1, keepdims=True) + EPS)
            hat = x * inv
            hat_ref[:, cols] = hat
            inv_ref[:, cols] = jnp.broadcast_to(inv, hat.shape)
            out_ref[:, cols] = (hat * gain_ref[h : h + 1, :]).astype(BF16)

    normalize(k_ref, gk_ref, khat, kinv, kn)
    send(KEY)
    normalize(q_ref, gq_ref, qhat, qinv, qn)
    send(QRY)
    send(COT)

    for slot, missing in ((LEFT, me == 0), (RIGHT, me == shards - 1)):

        @pl.when(missing)
        def _():
            for what in (KEY, VAL, QRY, COT):
                buf[slot, what] = jnp.zeros(buf.shape[2:], BF16)
            stat[slot] = jnp.zeros(stat.shape[1:], F32)

    def head(h):
        return pl.ds(pl.multiple_of(h * hd, hd), hd)

    reach = [reach_ref[b] for b in range(2)]
    picks = [[part_ref[b, lv] - peers[lv] * 2 for lv in range(LEVELS)] for b in range(2)]

    def one(flag):
        return jnp.where(flag, 1.0, 0.0).astype(F32)

    left_ok, right_ok = one(has_left), one(has_right)

    def score(b, first, count, weights):
        span = pl.ds(first * BLOCK, count * BLOCK)

        def body(h, carry):
            s = dot_t(qn[rows(b), head(h)], kcat[b, span, head(h)])
            gp = dot_t(g_ref[rows(b), head(h)], vcat[b, span, head(h)])
            e = jnp.exp2(s * log2e_scale)
            for i in range(count):
                w = weights[i]
                part = e[:, i * BLOCK : (i + 1) * BLOCK]
                if w is not None:
                    part = part * w
                e_s[2 * b + h, :, rows(first + i)] = part
            g_s[2 * b + h, :, span] = gp
            return carry

        lax.fori_loop(0, HEADS, body, 0)

    def place(b, pos, key, val):
        kcat[b, rows(pos), :] = key
        vcat[b, rows(pos), :] = val

    for b in range(2):
        for c in range(2):
            place(b, 2 - b + c, kn[rows(c), :], v_ref[rows(c), :])
        score(b, 2 - b, 2, [None if c == b else one(reach[b] >= 1) for c in range(2)])

    def blend(m, first, second):
        return (first.astype(F32) * (1.0 - m) + second.astype(F32) * m).astype(BF16)

    def partner_scores(level):
        slot = 2 + level
        arrived(slot, VAL)
        if slot == near:
            each_forward(VAL, lambda c: c.start())
        arrived(slot, KEY)
        if slot == near:
            each_forward(KEY, lambda c: c.start())
        for b in range(2):
            m = picks[b][level].astype(F32)
            place(
                b,
                2 * BAND + 1 + level,
                blend(m, buf[slot, KEY, rows(0), :], buf[slot, KEY, rows(1), :]),
                blend(m, buf[slot, VAL, rows(0), :], buf[slot, VAL, rows(1), :]),
            )
            score(b, 2 * BAND + 1 + level, 1, [None])

    partner_scores(0)
    partner_scores(1)
    partner_scores(3)
    for slot in (LEFT, RIGHT):
        arrived(slot, VAL)
        arrived(slot, KEY)
    two = [one(r >= 2) for r in reach]
    some = [one(r >= 1) for r in reach]
    for b, pos, c in ((0, 0, 0), (0, 1, 1), (1, 0, 1)):
        place(b, pos, buf[LEFT, KEY, rows(c), :], buf[LEFT, VAL, rows(c), :])
    score(0, 0, 2, [two[0] * left_ok, some[0] * left_ok])
    score(1, 0, 1, [two[1] * left_ok])
    for b, pos, c in ((0, 4, 0), (1, 3, 0), (1, 4, 1)):
        place(b, pos, buf[RIGHT, KEY, rows(c), :], buf[RIGHT, VAL, rows(c), :])
    score(0, 4, 1, [two[0] * right_ok])
    score(1, 3, 2, [some[1] * right_ok, two[1] * right_ok])
    partner_scores(2)

    lane = lax.broadcasted_iota(jnp.int32, (BLOCK, BLOCK), 1)
    packed = jnp.zeros((BLOCK, BLOCK), F32)
    for b in range(2):

        def finish(h, packed, b=b):
            at_row = 2 * b + h
            e = e_s[at_row]
            inv_total = 1.0 / jnp.sum(e, axis=-1, keepdims=True)
            out = (dot_n(e.astype(BF16), vcat[b, :, head(h)]) * inv_total).astype(BF16)
            o_ref[rows(b), head(h)] = out
            delta = jnp.sum(
                g_ref[rows(b), head(h)].astype(F32) * out.astype(F32), axis=-1, keepdims=True
            )
            ds = (e * inv_total * (g_s[at_row] - delta)).astype(BF16)
            grad = dot_n(ds, kcat[b, :, head(h)]) * scale
            s = grad * gq_ref[pl.ds(h, 1), :]
            hat = qhat[rows(b), head(h)]
            first = jnp.mean(s, axis=-1, keepdims=True)
            second = jnp.mean(s * hat, axis=-1, keepdims=True)
            dq_ref[rows(b), head(h)] = (
                (s - first - hat * second) * qinv[rows(b), head(h)]
            ).astype(BF16)
            packed = jnp.where(lane == at_row, inv_total, packed)
            return jnp.where(lane == 4 + at_row, delta, packed)

        packed = lax.fori_loop(0, HEADS, finish, packed)
    stats = packed.T[:8]
    own_stat[...] = stats
    width = (1, BLOCK)
    for slot in range(SLOTS):
        out_stat[slot, 0:8, :] = stats
        for b in range(2):
            if slot in (LEFT, RIGHT):
                first, second = two[b], some[b]
            else:
                first = second = picks[b][slot - 2].astype(F32)
            out_stat[slot, 8 + b : 9 + b, :] = jnp.broadcast_to(first, width)
            out_stat[slot, 10 + b : 11 + b, :] = jnp.broadcast_to(second, width)
        out_stat[slot, 12:16, :] = jnp.zeros((4, BLOCK), F32)
    send(STAT)

    if relay:
        for what in (QRY, COT):
            arrived(near, what)
            each_forward(what, lambda c: c.start())

    dk_acc[...] = jnp.zeros(dk_acc.shape, F32)
    dv_acc[...] = jnp.zeros(dv_acc.shape, F32)

    def terms(key, val, qry, cot, inv_total, delta):
        p = jnp.exp2(dot_t(key, qry) * log2e_scale) * inv_total
        ds = (p * (dot_t(val, cot) - delta)).astype(BF16)
        return dot_n(ds, qry), dot_n(p.astype(BF16), cot)

    def band_terms(pairs, qry_of, cot_of, stat_of):
        def body(h, carry):
            for b, c, row in pairs:
                inv_total = stat_of(2 * b + h)
                if row is not None:
                    inv_total = inv_total * stat_of(row)
                dk, dv = terms(
                    kn[rows(c), head(h)],
                    v_ref[rows(c), head(h)],
                    qry_of(b, h),
                    cot_of(b, h),
                    inv_total,
                    stat_of(4 + 2 * b + h),
                )
                dk_acc[rows(c), head(h)] += dk
                dv_acc[rows(c), head(h)] += dv
            return carry

        lax.fori_loop(0, HEADS, body, 0)

    def own_body(h, carry):
        for b in range(2):
            for c in range(2):
                inv_total = own_stat[pl.ds(2 * b + h, 1), :]
                if b != c:
                    inv_total = inv_total * some[b]
                dk, dv = terms(
                    kn[rows(c), head(h)],
                    v_ref[rows(c), head(h)],
                    qn[rows(b), head(h)],
                    g_ref[rows(b), head(h)],
                    inv_total,
                    own_stat[pl.ds(4 + 2 * b + h, 1), :],
                )
                dk_acc[rows(c), head(h)] += dk
                dv_acc[rows(c), head(h)] += dv
        return carry

    lax.fori_loop(0, HEADS, own_body, 0)

    def partner_terms(level):
        slot = 2 + level
        if slot != near:
            arrived(slot, QRY)
            arrived(slot, COT)
        arrived(slot, STAT)

        def body(h, carry):
            for b in range(2):
                m = stat[slot, 8 + b : 9 + b, :]
                dk, dv = terms(
                    blend(m, kn[rows(0), head(h)], kn[rows(1), head(h)]),
                    blend(m, v_ref[rows(0), head(h)], v_ref[rows(1), head(h)]),
                    buf[slot, QRY, rows(b), head(h)],
                    buf[slot, COT, rows(b), head(h)],
                    stat[slot, pl.ds(2 * b + h, 1), :],
                    stat[slot, pl.ds(4 + 2 * b + h, 1), :],
                )
                dk_acc[rows(0), head(h)] += dk * (1.0 - m)
                dk_acc[rows(1), head(h)] += dk * m
                dv_acc[rows(0), head(h)] += dv * (1.0 - m)
                dv_acc[rows(1), head(h)] += dv * m
            return carry

        lax.fori_loop(0, HEADS, body, 0)

    partner_terms(0)
    partner_terms(1)
    partner_terms(3)
    for slot, pairs in (
        (LEFT, ((1, 0, 11), (0, 0, 8), (1, 1, 9))),
        (RIGHT, ((0, 1, 10), (0, 0, 8), (1, 1, 9))),
    ):
        for what in (QRY, COT, STAT):
            arrived(slot, what)
        band_terms(
            pairs,
            lambda b, h, slot=slot: buf[slot, QRY, rows(b), head(h)],
            lambda b, h, slot=slot: buf[slot, COT, rows(b), head(h)],
            lambda r, slot=slot: stat[slot, pl.ds(r, 1), :],
        )
    partner_terms(2)

    for h in range(HEADS):
        cols = slice(h * hd, (h + 1) * hd)
        s = dk_acc[:, cols] * (scale * gk_ref[h : h + 1, :])
        hat = khat[:, cols]
        first = jnp.mean(s, axis=-1, keepdims=True)
        second = jnp.mean(s * hat, axis=-1, keepdims=True)
        dk_ref[:, cols] = ((s - first - hat * second) * kinv[:, cols]).astype(BF16)
        dv_ref[:, cols] = dv_acc[:, cols].astype(BF16)

    for what in (VAL, KEY, QRY, COT, STAT):
        each_copy(what, lambda c: c.wait_send())
    for what in (VAL, KEY, QRY, COT):
        each_forward(what, lambda c: c.wait_send())


def solution(mesh):
    shards = mesh.shape["grp"] * mesh.shape["ctx"]
    inner = mesh.shape["ctx"]

    def body(query_raw, key_raw, values, band_reach, partners, gain_query, gain_key, cotangent):
        n, width = query_raw.shape
        cat = POS * BLOCK
        vmem = pl.BlockSpec(memory_space=pltpu.VMEM)
        smem = pl.BlockSpec(memory_space=pltpu.SMEM)
        out = jax.ShapeDtypeStruct((n, width), BF16)
        return pl.pallas_call(
            functools.partial(kernel, shards, inner),
            out_shape=(out,) * 4,
            in_specs=[vmem] * 6 + [smem] * 2,
            out_specs=(vmem,) * 4,
            scratch_shapes=[
                pltpu.VMEM((SLOTS, 4, n, width), BF16),
                pltpu.VMEM((SLOTS, 16, BLOCK), F32),
                pltpu.VMEM((8, BLOCK), F32),
                pltpu.VMEM((SLOTS, 16, BLOCK), F32),
                pltpu.VMEM((n, width), BF16),
                pltpu.VMEM((n, width), BF16),
                pltpu.VMEM((n, width), F32),
                pltpu.VMEM((n, width), F32),
                pltpu.VMEM((n, width), F32),
                pltpu.VMEM((n, width), F32),
                pltpu.VMEM((2, cat, width), BF16),
                pltpu.VMEM((2, cat, width), BF16),
                pltpu.VMEM((2 * HEADS, BLOCK, cat), F32),
                pltpu.VMEM((2 * HEADS, BLOCK, cat), F32),
                pltpu.VMEM((n, width), F32),
                pltpu.VMEM((n, width), F32),
                pltpu.SemaphoreType.DMA((SLOTS, 5)),
                pltpu.SemaphoreType.DMA((SLOTS, 5)),
                pltpu.SemaphoreType.DMA((4,)),
            ],
            compiler_params=pltpu.CompilerParams(
                collective_id=0, has_side_effects=True, vmem_limit_bytes=40 * 2**20
            ),
        )(query_raw, key_raw, values, cotangent, gain_query, gain_key, band_reach, partners)

    seq = P(AXES, None)
    return jax.shard_map(
        body,
        mesh=mesh,
        in_specs=(seq, seq, seq, P(AXES), seq, P(), P(), seq),
        out_specs=(seq,) * 4,
        check_vma=False,
    )
```

time: 107 us -> 55 us (0.51)
  the two profiles are of different devices: /device:TPU:4 before, /device:TPU:1 now
where the time goes in v1:
time: 55 us; the launch traced here: 54.7 us
  Pallas kernels  45.2 us (82%)
  local copies, waits for them, and re-layouts  8.92 us (16%)
  between operations  0.66 us (1%)
    pallas_call x1, Pallas kernels, body(): pl.pallas_call(functools.partial(kernel, shards, inner), out_shape=(out,)...  45.2 us
    unnamed x20, local copies, waits for them, and re-layouts  8.92 us

profile of v1, /device:TPU:1, one launch (start us, length us, event | category | flops | bytes accessed | tf_op | source)
XLA Modules:
  0.0 54.7 jit_solution(12564224125303882328)
XLA Ops:
  0.6 0.0 copy-start
  0.6 0.9 %copy-done = bf16[256,256]{1,0:T(8,128)(2,1)S(1)} copy-done((bf16[256,256]{1,0:T(8,128)(2,1)S(1)}, bf16[256,256]{1,0:T(8,128)(2,1)}, u32[]{:S(2)}) %copy-start) | copy-done | bytes 131096
  1.5 0.0 copy-start.1
  1.5 0.9 %copy-done.1 = bf16[256,256]{1,0:T(8,128)(2,1)S(1)} copy-done((bf16[256,256]{1,0:T(8,128)(2,1)S(1)}, bf16[256,256]{1,0:T(8,128)(2,1)}, u32[]{:S(2)}) %copy-start.1) | copy-done | bytes 131096
  2.4 0.0 copy-start.2
  2.4 0.9 %copy-done.2 = bf16[256,256]{1,0:T(8,128)(2,1)S(1)} copy-done((bf16[256,256]{1,0:T(8,128)(2,1)S(1)}, bf16[256,256]{1,0:T(8,128)(2,1)}, u32[]{:S(2)}) %copy-start.2) | copy-done | bytes 131096
  3.3 0.0 copy-start.3
  3.4 0.9 %copy-done.3 = bf16[256,256]{1,0:T(8,128)(2,1)S(1)} copy-done((bf16[256,256]{1,0:T(8,128)(2,1)S(1)}, bf16[256,256]{1,0:T(8,128)(2,1)}, u32[]{:S(2)}) %copy-start.3) | copy-done | bytes 131096
  4.3 0.0 copy-start.4
  4.3 0.7 %copy-done.4 = f32[2,128]{1,0:T(2,128)S(1)} copy-done((f32[2,128]{1,0:T(2,128)S(1)}, f32[2,128]{1,0:T(2,128)}, u32[]{:S(2)}) %copy-start.4) | copy-done | bytes 1048
  4.9 0.0 copy-start.5
  4.9 0.7 %copy-done.5 = f32[2,128]{1,0:T(2,128)S(1)} copy-done((f32[2,128]{1,0:T(2,128)S(1)}, f32[2,128]{1,0:T(2,128)}, u32[]{:S(2)}) %copy-start.5) | copy-done | bytes 1048
  5.6 0.0 copy-start.6
  5.6 0.7 %copy-done.6 = s32[2,4]{1,0:T(2,128)S(1)} copy-done((s32[2,4]{1,0:T(2,128)S(1)}, s32[2,4]{1,0:T(2,128)}, u32[]{:S(2)}) %copy-start.6) | copy-done | bytes 56
  6.3 0.0 copy-start.7
  6.3 0.7 %copy-done.7 = s32[2]{0:T(128)S(1)} copy-done((s32[2]{0:T(128)S(1)}, s32[2]{0:T(128)}, u32[]{:S(2)}) %copy-start.7) | copy-done | bytes 32
  6.9 45.2 %shard_map.111 = (bf16[256,256]{1,0:T(8,128)(2,1)S(1)}, bf16[256,256]{1,0:T(8,128)(2,1)S(1)}, bf16[256,256]{1,0:T(8,128)(2,1)S(1)}, bf16[256,256]{1,0:T(8,128)(2,1)S(1)}) custom-call(bf16[256,256]{1,0:T(8,128)(2,1)S(1)} %copy-done, bf16[256,256]{1,0:T(8,128)(2,1)S(1)} %copy-done.1, bf16[256,256]{1,0:T(8,128)(2,1)S(1)} %copy-done.2, ...), custom_call_target="tpu_custom_call" | custom-call | tf_op jit(solution)/shard_map/pallas_call | solution.py:448
  52.1 0.7 %copy.16 = bf16[256,256]{1,0:T(8,128)(2,1)} copy(bf16[256,256]{1,0:T(8,128)(2,1)S(1)} %get-tuple-element.8) | data formatting | bytes 262144
  52.8 0.7 %copy.17 = bf16[256,256]{1,0:T(8,128)(2,1)} copy(bf16[256,256]{1,0:T(8,128)(2,1)S(1)} %get-tuple-element.9) | data formatting | bytes 262144
  53.4 0.7 %copy.18 = bf16[256,256]{1,0:T(8,128)(2,1)} copy(bf16[256,256]{1,0:T(8,128)(2,1)S(1)} %get-tuple-element.10) | data formatting | bytes 262144
  54.1 0.7 %copy.19 = bf16[256,256]{1,0:T(8,128)(2,1)} copy(bf16[256,256]{1,0:T(8,128)(2,1)S(1)} %get-tuple-element.11) | data formatting | bytes 262144
Async XLA Ops:
  0.6 0.9 %copy-start = (bf16[256,256]{1,0:T(8,128)(2,1)S(1)}, bf16[256,256]{1,0:T(8,128)(2,1)}, u32[]{:S(2)}) copy-start(bf16[256,256]{1,0:T(8,128)(2,1)} %q_ref.1) | copy-start | bytes 393220
  1.5 0.9 %copy-start.1 = (bf16[256,256]{1,0:T(8,128)(2,1)S(1)}, bf16[256,256]{1,0:T(8,128)(2,1)}, u32[]{:S(2)}) copy-start(bf16[256,256]{1,0:T(8,128)(2,1)} %k_ref.1) | copy-start | bytes 393220
  2.4 0.9 %copy-start.2 = (bf16[256,256]{1,0:T(8,128)(2,1)S(1)}, bf16[256,256]{1,0:T(8,128)(2,1)}, u32[]{:S(2)}) copy-start(bf16[256,256]{1,0:T(8,128)(2,1)} %v_ref.1) | copy-start | bytes 393220
  3.3 0.9 %copy-start.3 = (bf16[256,256]{1,0:T(8,128)(2,1)S(1)}, bf16[256,256]{1,0:T(8,128)(2,1)}, u32[]{:S(2)}) copy-start(bf16[256,256]{1,0:T(8,128)(2,1)} %g_ref.1) | copy-start | bytes 393220
  4.3 0.7 %copy-start.4 = (f32[2,128]{1,0:T(2,128)S(1)}, f32[2,128]{1,0:T(2,128)}, u32[]{:S(2)}) copy-start(f32[2,128]{1,0:T(2,128)} %gq_ref.1) | copy-start | bytes 3076
  4.9 0.7 %copy-start.5 = (f32[2,128]{1,0:T(2,128)S(1)}, f32[2,128]{1,0:T(2,128)}, u32[]{:S(2)}) copy-start(f32[2,128]{1,0:T(2,128)} %gk_ref.1) | copy-start | bytes 3076
  5.6 0.7 %copy-start.6 = (s32[2,4]{1,0:T(2,128)S(1)}, s32[2,4]{1,0:T(2,128)}, u32[]{:S(2)}) copy-start(s32[2,4]{1,0:T(2,128)} %part_ref.1) | copy-start | bytes 100
  6.3 0.7 %copy-start.7 = (s32[2]{0:T(128)S(1)}, s32[2]{0:T(128)}, u32[]{:S(2)}) copy-start(s32[2]{0:T(128)} %reach_ref.1) | copy-start | bytes 28

commit v2 on v1

--- a/solution.py
+++ b/solution.py
@@ -38,18 +38,30 @@
 def kernel(
     shards,
     inner,
-    q_ref,
-    k_ref,
-    v_ref,
-    g_ref,
-    gq_ref,
-    gk_ref,
-    reach_ref,
-    part_ref,
+    v_in,
+    k_in,
+    gk_in,
+    q_in,
+    gq_in,
+    g_in,
+    reach_in,
+    part_in,
+    o_out,
+    dq_out,
+    dk_out,
+    dv_out,
     o_ref,
     dq_ref,
     dk_ref,
     dv_ref,
+    v_ref,
+    k_ref,
+    gk_ref,
+    q_ref,
+    gq_ref,
+    g_ref,
+    reach_ref,
+    part_ref,
     buf,
     stat,
     own_stat,
@@ -69,7 +81,33 @@
     send_sem,
     recv_sem,
     fwd_sem,
+    far_sem,
+    in_sem,
+    out_sem,
 ):
+    loads = [
+        pltpu.make_async_copy(src, dst, in_sem.at[i])
+        for i, (src, dst) in enumerate(
+            (
+                (v_in, v_ref),
+                (k_in, k_ref),
+                (gk_in, gk_ref),
+                (q_in, q_ref),
+                (gq_in, gq_ref),
+                (g_in, g_ref),
+                (reach_in, reach_ref),
+                (part_in, part_ref),
+            )
+        )
+    ]
+    for load in loads:
+        load.start()
+    stores = [
+        pltpu.make_async_copy(src, dst, out_sem.at[i])
+        for i, (src, dst) in enumerate(
+            ((o_ref, o_out), (dq_ref, dq_out), (dk_ref, dk_out), (dv_ref, dv_out))
+        )
+    ]
     me = lax.axis_index(AXES)
     hd = gq_ref.shape[1]
     scale = hd ** (-0.5)
@@ -77,10 +115,13 @@
     masks = [shards >> (level + 1) for level in range(LEVELS)]
     relay = 2 in masks
     near = 2 + masks.index(2) if relay else None
+    chain = relay and 4 in masks
+    far = 2 + masks.index(4) if chain else None
     has_left = me > 0
     has_right = me < shards - 1
     core = lax.rem(me, 2)
     chip_odd = lax.rem(me // 2, 2)
+    place_in_8 = lax.rem(me, 8)
     peers = [jnp.bitwise_xor(me, m) for m in masks]
 
     def at(t):
@@ -98,8 +139,31 @@
     def _():
         pl.semaphore_signal(barrier, inc=1, device_id=at(me + 1), device_id_type=MESH)
 
+    if chain:
+
+        @pl.when(place_in_8 == 3)
+        def _():
+            pl.semaphore_signal(barrier, inc=1, device_id=at(me - 3), device_id_type=MESH)
+
+        @pl.when(place_in_8 == 0)
+        def _():
+            pl.semaphore_signal(barrier, inc=1, device_id=at(me + 3), device_id_type=MESH)
+
+        @pl.when(place_in_8 == 4)
+        def _():
+            pl.semaphore_signal(barrier, inc=1, device_id=at(me + 3), device_id_type=MESH)
+
+        @pl.when(place_in_8 == 7)
+        def _():
+            pl.semaphore_signal(barrier, inc=1, device_id=at(me - 3), device_id_type=MESH)
+
+        extra = (
+            (lax.rem(place_in_8, 4) == 0) | (lax.rem(place_in_8, 4) == 3)
+        ).astype(jnp.int32)
+    else:
+        extra = 0
     pl.semaphore_wait(
-        barrier, LEVELS + has_left.astype(jnp.int32) + has_right.astype(jnp.int32)
+        barrier, extra + LEVELS + has_left.astype(jnp.int32) + has_right.astype(jnp.int32)
     )
 
     sources = {KEY: kn, VAL: v_ref, QRY: qn, COT: g_ref}
@@ -139,16 +203,22 @@
         return has_left
 
     def each_copy(what, act):
+        @pl.when(to_right(what))
+        def _():
+            act(copy(LEFT, what, me + 1))
+
+        @pl.when(to_left(what))
+        def _():
+            act(copy(RIGHT, what, me - 1))
+
         for level in reversed(range(LEVELS)):
-            act(copy(2 + level, what, peers[level]))
-
-        @pl.when(to_right(what))
-        def _():
-            act(copy(LEFT, what, me + 1))
-
-        @pl.when(to_left(what))
-        def _():
-            act(copy(RIGHT, what, me - 1))
+            if 2 + level == far and what != STAT:
+
+                @pl.when((place_in_8 != 3) & (place_in_8 != 4))
+                def _(level=level):
+                    act(copy(2 + level, what, peers[level]))
+            else:
+                act(copy(2 + level, what, peers[level]))
 
     def send(what):
         each_copy(what, lambda c: c.start())
@@ -179,8 +249,38 @@
         def _():
             act(forward(LEFT, what, me - 1))
 
+    def chained(what, act):
+        if not chain:
+            return
+
+        def hop(slot, t):
+            return pltpu.make_async_remote_copy(
+                src_ref=buf.at[slot, what],
+                dst_ref=buf.at[far, what],
+                send_sem=far_sem.at[what],
+                recv_sem=recv_sem.at[far, what],
+                device_id=at(t),
+                device_id_type=MESH,
+            )
+
+        @pl.when(place_in_8 == 3)
+        def _():
+            act(hop(RIGHT, me - 3))
+
+        @pl.when(place_in_8 == 4)
+        def _():
+            act(hop(LEFT, me + 3))
+
+    def pass_on(what):
+        if relay:
+            arrived(near, what)
+            each_forward(what, lambda c: c.start())
+        arrived(LEFT, what)
+        arrived(RIGHT, what)
+        chained(what, lambda c: c.start())
+
+    loads[0].wait()
     send(VAL)
-
     def normalize(x_ref, gain_ref, hat_ref, inv_ref, out_ref):
         for h in range(HEADS):
             cols = slice(h * hd, (h + 1) * hd)
@@ -192,11 +292,18 @@
             inv_ref[:, cols] = jnp.broadcast_to(inv, hat.shape)
             out_ref[:, cols] = (hat * gain_ref[h : h + 1, :]).astype(BF16)
 
+    loads[1].wait()
+    loads[2].wait()
     normalize(k_ref, gk_ref, khat, kinv, kn)
     send(KEY)
+    loads[3].wait()
+    loads[4].wait()
     normalize(q_ref, gq_ref, qhat, qinv, qn)
     send(QRY)
+    loads[5].wait()
     send(COT)
+    loads[6].wait()
+    loads[7].wait()
 
     for slot, missing in ((LEFT, me == 0), (RIGHT, me == shards - 1)):
 
@@ -249,12 +356,9 @@
 
     def partner_scores(level):
         slot = 2 + level
-        arrived(slot, VAL)
-        if slot == near:
-            each_forward(VAL, lambda c: c.start())
-        arrived(slot, KEY)
-        if slot == near:
-            each_forward(KEY, lambda c: c.start())
+        if slot != near:
+            arrived(slot, VAL)
+            arrived(slot, KEY)
         for b in range(2):
             m = picks[b][level].astype(F32)
             place(
@@ -267,10 +371,9 @@
 
     partner_scores(0)
     partner_scores(1)
+    pass_on(VAL)
+    pass_on(KEY)
     partner_scores(3)
-    for slot in (LEFT, RIGHT):
-        arrived(slot, VAL)
-        arrived(slot, KEY)
     two = [one(r >= 2) for r in reach]
     some = [one(r >= 1) for r in reach]
     for b, pos, c in ((0, 0, 0), (0, 1, 1), (1, 0, 1)):
@@ -323,11 +426,10 @@
             out_stat[slot, 10 + b : 11 + b, :] = jnp.broadcast_to(second, width)
         out_stat[slot, 12:16, :] = jnp.zeros((4, BLOCK), F32)
     send(STAT)
-
-    if relay:
-        for what in (QRY, COT):
-            arrived(near, what)
-            each_forward(what, lambda c: c.start())
+    stores[0].start()
+    stores[1].start()
+
+    pass_on(QRY)
 
     dk_acc[...] = jnp.zeros(dk_acc.shape, F32)
     dv_acc[...] = jnp.zeros(dv_acc.shape, F32)
@@ -405,13 +507,13 @@
 
     partner_terms(0)
     partner_terms(1)
+    pass_on(COT)
     partner_terms(3)
     for slot, pairs in (
         (LEFT, ((1, 0, 11), (0, 0, 8), (1, 1, 9))),
         (RIGHT, ((0, 1, 10), (0, 0, 8), (1, 1, 9))),
     ):
-        for what in (QRY, COT, STAT):
-            arrived(slot, what)
+        arrived(slot, STAT)
         band_terms(
             pairs,
             lambda b, h, slot=slot: buf[slot, QRY, rows(b), head(h)],
@@ -420,6 +522,8 @@
         )
     partner_terms(2)
 
+    dv_ref[...] = dv_acc[...].astype(BF16)
+    stores[3].start()
     for h in range(HEADS):
         cols = slice(h * hd, (h + 1) * hd)
         s = dk_acc[:, cols] * (scale * gk_ref[h : h + 1, :])
@@ -427,12 +531,32 @@
         first = jnp.mean(s, axis=-1, keepdims=True)
         second = jnp.mean(s * hat, axis=-1, keepdims=True)
         dk_ref[:, cols] = ((s - first - hat * second) * kinv[:, cols]).astype(BF16)
-        dv_ref[:, cols] = dv_acc[:, cols].astype(BF16)
+    stores[2].start()
 
     for what in (VAL, KEY, QRY, COT, STAT):
         each_copy(what, lambda c: c.wait_send())
     for what in (VAL, KEY, QRY, COT):
         each_forward(what, lambda c: c.wait_send())
+        chained(what, lambda c: c.wait_send())
+    for store in stores:
+        store.wait()
+
+
+def hand_on(*refs):
+    count = (len(refs) - 2) // 3
+    in_sem, out_sem = refs[-2:]
+    held = refs[2 * count : 3 * count]
+    loads = [pltpu.make_async_copy(refs[i], held[i], in_sem.at[i]) for i in range(count)]
+    stores = [
+        pltpu.make_async_copy(held[i], refs[count + i], out_sem.at[i]) for i in range(count)
+    ]
+    for c in loads:
+        c.start()
+    for load, store in zip(loads, stores):
+        load.wait()
+        store.start()
+    for c in stores:
+        c.wait()
 
 
 def solution(mesh):
@@ -442,15 +566,26 @@
     def body(query_raw, key_raw, values, band_reach, partners, gain_query, gain_key, cotangent):
         n, width = query_raw.shape
         cat = POS * BLOCK
-        vmem = pl.BlockSpec(memory_space=pltpu.VMEM)
-        smem = pl.BlockSpec(memory_space=pltpu.SMEM)
+        hbm = pl.BlockSpec(memory_space=pltpu.HBM)
         out = jax.ShapeDtypeStruct((n, width), BF16)
-        return pl.pallas_call(
+        results = pl.pallas_call(
             functools.partial(kernel, shards, inner),
             out_shape=(out,) * 4,
-            in_specs=[vmem] * 6 + [smem] * 2,
-            out_specs=(vmem,) * 4,
+            in_specs=[hbm] * 8,
+            out_specs=(hbm,) * 4,
             scratch_shapes=[
+                pltpu.VMEM((n, width), BF16),
+                pltpu.VMEM((n, width), BF16),
+                pltpu.VMEM((n, width), BF16),
+                pltpu.VMEM((n, width), BF16),
+                pltpu.VMEM((n, width), BF16),
+                pltpu.VMEM((n, width), BF16),
+                pltpu.VMEM(gain_key.shape, F32),
+                pltpu.VMEM((n, width), BF16),
+                pltpu.VMEM(gain_query.shape, F32),
+                pltpu.VMEM((n, width), BF16),
+                pltpu.SMEM(band_reach.shape, jnp.int32),
+                pltpu.SMEM(partners.shape, jnp.int32),
                 pltpu.VMEM((SLOTS, 4, n, width), BF16),
                 pltpu.VMEM((SLOTS, 16, BLOCK), F32),
                 pltpu.VMEM((8, BLOCK), F32),
@@ -470,11 +605,22 @@
                 pltpu.SemaphoreType.DMA((SLOTS, 5)),
                 pltpu.SemaphoreType.DMA((SLOTS, 5)),
                 pltpu.SemaphoreType.DMA((4,)),
+                pltpu.SemaphoreType.DMA((4,)),
+                pltpu.SemaphoreType.DMA((8,)),
+                pltpu.SemaphoreType.DMA((4,)),
             ],
             compiler_params=pltpu.CompilerParams(
-                collective_id=0, has_side_effects=True, vmem_limit_bytes=40 * 2**20
+                collective_id=0, has_side_effects=True, vmem_limit_bytes=64 * 2**20
             ),
-        )(query_raw, key_raw, values, cotangent, gain_query, gain_key, band_reach, partners)
+        )(values, key_raw, gain_key, query_raw, gain_query, cotangent, band_reach, partners)
+        return pl.pallas_call(
+            hand_on,
+            out_shape=(out,) * 4,
+            in_specs=[hbm] * 4,
+            out_specs=(hbm,) * 4,
+            scratch_shapes=[pltpu.VMEM((n, width), BF16)] * 4
+            + [pltpu.SemaphoreType.DMA((4,))] * 2,
+        )(*results)
 
     seq = P(AXES, None)
     return jax.shard_map(

time: 55 us -> 48.2 us (0.88)
  local copies, waits for them, and re-layouts: 8.92 us -> 0 us
  Pallas kernels: 45.2 us -> 47.4 us
    unnamed x20 -> x0, local copies, waits for them, and re-layouts: 8.92 us -> none
    pallas_call x0 -> x1, Pallas kernels: none -> 1.82 us  [body(): pl.pallas_call(hand_on, out_shape=(out,) * 4, in_specs=[hbm] * 4, out_spe...]
where the time goes in v2:
time: 48.2 us; the launch traced here: 48.1 us
  Pallas kernels  47.4 us (98%)
  between operations  0.64 us (1%)
    pallas_call x1, Pallas kernels, body(): pl.pallas_call(functools.partial(kernel, shards, inner), out_shape=(out,)...  45.6 us
    pallas_call x1, Pallas kernels, body(): pl.pallas_call(hand_on, out_shape=(out,) * 4, in_specs=[hbm] * 4, out_spe...  1.82 us

profile of v2, /device:TPU:1, one launch (start us, length us, event | category | flops | bytes accessed | tf_op | source)
XLA Modules:
  0.0 48.1 jit_solution(1125466775772369597)
XLA Ops:
  0.6 45.6 %shard_map.111 = (bf16[256,256]{1,0:T(8,128)(2,1)}, bf16[256,256]{1,0:T(8,128)(2,1)}, bf16[256,256]{1,0:T(8,128)(2,1)}, bf16[256,256]{1,0:T(8,128)(2,1)}) custom-call(bf16[256,256]{1,0:T(8,128)(2,1)} %v_in.1, bf16[256,256]{1,0:T(8,128)(2,1)} %k_in.1, f32[2,128]{1,0:T(2,128)} %gk_in.1, bf16[256,256]{1,0:T(8,128)(2,1)} %q_in.1, f32[2,128]{1,0:T(2,128)} %gq_in.1, ...), custom_call_target="tpu_custom_call" | custom-call | tf_op jit(solution)/shard_map/pallas_call | solution.py:571
  46.3 1.8 %shard_map.112 = (bf16[256,256]{1,0:T(8,128)(2,1)}, bf16[256,256]{1,0:T(8,128)(2,1)}, bf16[256,256]{1,0:T(8,128)(2,1)}, bf16[256,256]{1,0:T(8,128)(2,1)}) custom-call(bf16[256,256]{1,0:T(8,128)(2,1)} %get-tuple-element.8.refs_0_, bf16[256,256]{1,0:T(8,128)(2,1)} %get-tuple-element.9.refs_1_, bf16[256,256]{1,0:T(8,128)(2,1)} %get-tuple-element.10.refs_2_, ...), custom_call_target="tpu_custom_call" | custom-call | tf_op jit(solution)/shard_map/pallas_call | solution.py:616

commit v3 on v2

--- a/solution.py
+++ b/solution.py
@@ -21,6 +21,8 @@
 SLOTS = 2 + LEVELS
 KEY, VAL, QRY, COT, STAT = 0, 1, 2, 3, 4
 POS = 2 * BAND + 1 + LEVELS
+RELAYED = (KEY, VAL, QRY, COT)
+CHAINED = (KEY, VAL, QRY, COT)
 
 
 def dot_t(a, b):
@@ -193,12 +195,12 @@
         )
 
     def to_right(what):
-        if relay and what != STAT:
+        if relay and what in RELAYED:
             return has_right & ((core == 0) | (chip_odd == 1))
         return has_right
 
     def to_left(what):
-        if relay and what != STAT:
+        if relay and what in RELAYED:
             return has_left & ((core == 1) | (chip_odd == 0))
         return has_left
 
@@ -212,7 +214,7 @@
             act(copy(RIGHT, what, me - 1))
 
         for level in reversed(range(LEVELS)):
-            if 2 + level == far and what != STAT:
+            if 2 + level == far and what in CHAINED:
 
                 @pl.when((place_in_8 != 3) & (place_in_8 != 4))
                 def _(level=level):
@@ -238,7 +240,7 @@
             copy(slot, what, peers[slot - 2]).wait_recv()
 
     def each_forward(what, act):
-        if not relay:
+        if not relay or what not in RELAYED:
             return
 
         @pl.when((core == 0) & (chip_odd == 0))
@@ -250,7 +252,7 @@
             act(forward(LEFT, what, me - 1))
 
     def chained(what, act):
-        if not chain:
+        if not chain or what not in CHAINED:
             return
 
         def hop(slot, t):
@@ -271,10 +273,12 @@
         def _():
             act(hop(LEFT, me + 3))
 
-    def pass_on(what):
+    def pass_near(what):
         if relay:
             arrived(near, what)
             each_forward(what, lambda c: c.start())
+
+    def pass_far(what):
         arrived(LEFT, what)
         arrived(RIGHT, what)
         chained(what, lambda c: c.start())
@@ -340,7 +344,7 @@
             g_s[2 * b + h, :, span] = gp
             return carry
 
-        lax.fori_loop(0, HEADS, body, 0)
+        lax.fori_loop(0, HEADS, body, 0, unroll=True)
 
     def place(b, pos, key, val):
         kcat[b, rows(pos), :] = key
@@ -369,10 +373,12 @@
             )
             score(b, 2 * BAND + 1 + level, 1, [None])
 
+    pass_near(VAL)
     partner_scores(0)
+    pass_far(VAL)
+    pass_near(KEY)
     partner_scores(1)
-    pass_on(VAL)
-    pass_on(KEY)
+    pass_far(KEY)
     partner_scores(3)
     two = [one(r >= 2) for r in reach]
     some = [one(r >= 1) for r in reach]
@@ -411,7 +417,7 @@
             packed = jnp.where(lane == at_row, inv_total, packed)
             return jnp.where(lane == 4 + at_row, delta, packed)
 
-        packed = lax.fori_loop(0, HEADS, finish, packed)
+        packed = lax.fori_loop(0, HEADS, finish, packed, unroll=True)
     stats = packed.T[:8]
     own_stat[...] = stats
     width = (1, BLOCK)
@@ -429,7 +435,6 @@
     stores[0].start()
     stores[1].start()
 
-    pass_on(QRY)
 
     dk_acc[...] = jnp.zeros(dk_acc.shape, F32)
     dv_acc[...] = jnp.zeros(dv_acc.shape, F32)
@@ -457,7 +462,7 @@
                 dv_acc[rows(c), head(h)] += dv
             return carry
 
-        lax.fori_loop(0, HEADS, body, 0)
+        lax.fori_loop(0, HEADS, body, 0, unroll=True)
 
     def own_body(h, carry):
         for b in range(2):
@@ -477,7 +482,7 @@
                 dv_acc[rows(c), head(h)] += dv
         return carry
 
-    lax.fori_loop(0, HEADS, own_body, 0)
+    lax.fori_loop(0, HEADS, own_body, 0, unroll=True)
 
     def partner_terms(level):
         slot = 2 + level
@@ -503,11 +508,14 @@
                 dv_acc[rows(1), head(h)] += dv * m
             return carry
 
-        lax.fori_loop(0, HEADS, body, 0)
-
+        lax.fori_loop(0, HEADS, body, 0, unroll=True)
+
+    pass_near(QRY)
+    pass_far(QRY)
     partner_terms(0)
     partner_terms(1)
-    pass_on(COT)
+    pass_near(COT)
+    pass_far(COT)
     partner_terms(3)
     for slot, pairs in (
         (LEFT, ((1, 0, 11), (0, 0, 8), (1, 1, 9))),

time: 48.2 us -> 45.4 us (0.942)
  Pallas kernels: 47.4 us -> 44.6 us
    pallas_call x1, Pallas kernels: 45.6 us -> 42.8 us  [body(): pl.pallas_call(functools.partial(kernel, shards, inner), out_shape=(out,)...]
where the time goes in v3:
time: 45.4 us; the launch traced here: 45.3 us
  Pallas kernels  44.6 us (98%)
  between operations  0.64 us (1%)
    pallas_call x1, Pallas kernels, body(): pl.pallas_call(functools.partial(kernel, shards, inner), out_shape=(out,)...  42.8 us
    pallas_call x1, Pallas kernels, body(): pl.pallas_call(hand_on, out_shape=(out,) * 4, in_specs=[hbm] * 4, out_spe...  1.82 us

profile of v3, /device:TPU:1, one launch (start us, length us, event | category | flops | bytes accessed | tf_op | source)
XLA Modules:
  0.0 45.3 jit_solution(10987677101471341567)
XLA Ops:
  0.6 42.8 %shard_map.111 = (bf16[256,256]{1,0:T(8,128)(2,1)}, bf16[256,256]{1,0:T(8,128)(2,1)}, bf16[256,256]{1,0:T(8,128)(2,1)}, bf16[256,256]{1,0:T(8,128)(2,1)}) custom-call(bf16[256,256]{1,0:T(8,128)(2,1)} %v_in.1, bf16[256,256]{1,0:T(8,128)(2,1)} %k_in.1, f32[2,128]{1,0:T(2,128)} %gk_in.1, bf16[256,256]{1,0:T(8,128)(2,1)} %q_in.1, f32[2,128]{1,0:T(2,128)} %gq_in.1, ...), custom_call_target="tpu_custom_call" | custom-call | tf_op jit(solution)/shard_map/pallas_call | solution.py:579
  43.4 1.8 %shard_map.112 = (bf16[256,256]{1,0:T(8,128)(2,1)}, bf16[256,256]{1,0:T(8,128)(2,1)}, bf16[256,256]{1,0:T(8,128)(2,1)}, bf16[256,256]{1,0:T(8,128)(2,1)}) custom-call(bf16[256,256]{1,0:T(8,128)(2,1)} %get-tuple-element.8.refs_0_, bf16[256,256]{1,0:T(8,128)(2,1)} %get-tuple-element.9.refs_1_, bf16[256,256]{1,0:T(8,128)(2,1)} %get-tuple-element.10.refs_2_, ...), custom_call_target="tpu_custom_call" | custom-call | tf_op jit(solution)/shard_map/pallas_call | solution.py:624

commit v4 on v3

--- a/solution.py
+++ b/solution.py
@@ -80,6 +80,8 @@
     g_s,
     dk_acc,
     dv_acc,
+    ahead_s,
+    partner_s,
     send_sem,
     recv_sem,
     fwd_sem,
@@ -439,14 +441,23 @@
     dk_acc[...] = jnp.zeros(dk_acc.shape, F32)
     dv_acc[...] = jnp.zeros(dv_acc.shape, F32)
 
-    def terms(key, val, qry, cot, inv_total, delta):
-        p = jnp.exp2(dot_t(key, qry) * log2e_scale) * inv_total
+    def terms(key, val, qry, cot, inv_total, delta, e=None):
+        if e is None:
+            e = jnp.exp2(dot_t(key, qry) * log2e_scale)
+        p = e * inv_total
         ds = (p * (dot_t(val, cot) - delta)).astype(BF16)
         return dot_n(ds, qry), dot_n(p.astype(BF16), cot)
 
-    def band_terms(pairs, qry_of, cot_of, stat_of):
+    def ahead(slot, pairs):
+        for h in range(HEADS):
+            cols = slice(h * hd, (h + 1) * hd)
+            for i, (b, c, _) in enumerate(pairs):
+                s = dot_t(kn[rows(c), cols], buf[slot, QRY, rows(b), cols])
+                ahead_s[slot, i, h] = jnp.exp2(s * log2e_scale)
+
+    def band_terms(slot, pairs, qry_of, cot_of, stat_of):
         def body(h, carry):
-            for b, c, row in pairs:
+            for i, (b, c, row) in enumerate(pairs):
                 inv_total = stat_of(2 * b + h)
                 if row is not None:
                     inv_total = inv_total * stat_of(row)
@@ -457,6 +468,7 @@
                     cot_of(b, h),
                     inv_total,
                     stat_of(4 + 2 * b + h),
+                    ahead_s[slot, i, h],
                 )
                 dk_acc[rows(c), head(h)] += dk
                 dv_acc[rows(c), head(h)] += dv
@@ -484,12 +496,26 @@
 
     lax.fori_loop(0, HEADS, own_body, 0, unroll=True)
 
-    def partner_terms(level):
+    def partner_ahead(level):
         slot = 2 + level
         if slot != near:
             arrived(slot, QRY)
+        arrived(slot, STAT)
+        for h in range(HEADS):
+            cols = slice(h * hd, (h + 1) * hd)
+            for b in range(2):
+                m = stat[slot, 8 + b : 9 + b, :]
+                key = blend(m, kn[rows(0), cols], kn[rows(1), cols])
+                s = dot_t(key, buf[slot, QRY, rows(b), cols])
+                partner_s[level - 2, b, h] = jnp.exp2(s * log2e_scale)
+
+    def partner_terms(level):
+        slot = 2 + level
+        if level < 2:
+            arrived(slot, QRY)
+            arrived(slot, STAT)
+        if slot != near:
             arrived(slot, COT)
-        arrived(slot, STAT)
 
         def body(h, carry):
             for b in range(2):
@@ -501,6 +527,7 @@
                     buf[slot, COT, rows(b), head(h)],
                     stat[slot, pl.ds(2 * b + h, 1), :],
                     stat[slot, pl.ds(4 + 2 * b + h, 1), :],
+                    partner_s[level - 2, b, h] if level >= 2 else None,
                 )
                 dk_acc[rows(0), head(h)] += dk * (1.0 - m)
                 dk_acc[rows(1), head(h)] += dk * m
@@ -514,15 +541,21 @@
     pass_far(QRY)
     partner_terms(0)
     partner_terms(1)
+    band_pairs = (
+        (LEFT, ((1, 0, 11), (0, 0, 8), (1, 1, 9))),
+        (RIGHT, ((0, 1, 10), (0, 0, 8), (1, 1, 9))),
+    )
+    for slot, pairs in band_pairs:
+        ahead(slot, pairs)
+    partner_ahead(3)
+    partner_ahead(2)
     pass_near(COT)
     pass_far(COT)
     partner_terms(3)
-    for slot, pairs in (
-        (LEFT, ((1, 0, 11), (0, 0, 8), (1, 1, 9))),
-        (RIGHT, ((0, 1, 10), (0, 0, 8), (1, 1, 9))),
-    ):
+    for slot, pairs in band_pairs:
         arrived(slot, STAT)
         band_terms(
+            slot,
             pairs,
             lambda b, h, slot=slot: buf[slot, QRY, rows(b), head(h)],
             lambda b, h, slot=slot: buf[slot, COT, rows(b), head(h)],
@@ -610,6 +643,8 @@
                 pltpu.VMEM((2 * HEADS, BLOCK, cat), F32),
                 pltpu.VMEM((n, width), F32),
                 pltpu.VMEM((n, width), F32),
+                pltpu.VMEM((2, 3, HEADS, BLOCK, BLOCK), F32),
+                pltpu.VMEM((2, 2, HEADS, BLOCK, BLOCK), F32),
                 pltpu.SemaphoreType.DMA((SLOTS, 5)),
                 pltpu.SemaphoreType.DMA((SLOTS, 5)),
                 pltpu.SemaphoreType.DMA((4,)),

time: 45.4 us -> 44.6 us (0.982)
  Pallas kernels: 44.6 us -> 43.8 us
    pallas_call x1, Pallas kernels: 42.8 us -> 42 us  [body(): pl.pallas_call(functools.partial(kernel, shards, inner), out_shape=(out,)...]
where the time goes in v4:
time: 44.6 us; the launch traced here: 44.5 us
  Pallas kernels  43.8 us (98%)
  between operations  0.64 us (1%)
    pallas_call x1, Pallas kernels, body(): pl.pallas_call(functools.partial(kernel, shards, inner), out_shape=(out,)...  42 us
    pallas_call x1, Pallas kernels, body(): pl.pallas_call(hand_on, out_shape=(out,) * 4, in_specs=[hbm] * 4, out_spe...  1.82 us

profile of v4, /device:TPU:1, one launch (start us, length us, event | category | flops | bytes accessed | tf_op | source)
XLA Modules:
  0.0 44.5 jit_solution(8462016754566263571)
XLA Ops:
  0.6 42.0 %shard_map.111 = (bf16[256,256]{1,0:T(8,128)(2,1)}, bf16[256,256]{1,0:T(8,128)(2,1)}, bf16[256,256]{1,0:T(8,128)(2,1)}, bf16[256,256]{1,0:T(8,128)(2,1)}) custom-call(bf16[256,256]{1,0:T(8,128)(2,1)} %v_in.1, bf16[256,256]{1,0:T(8,128)(2,1)} %k_in.1, f32[2,128]{1,0:T(2,128)} %gk_in.1, bf16[256,256]{1,0:T(8,128)(2,1)} %q_in.1, f32[2,128]{1,0:T(2,128)} %gq_in.1, ...), custom_call_target="tpu_custom_call" | custom-call | tf_op jit(solution)/shard_map/pallas_call | solution.py:612
  42.7 1.8 %shard_map.112 = (bf16[256,256]{1,0:T(8,128)(2,1)}, bf16[256,256]{1,0:T(8,128)(2,1)}, bf16[256,256]{1,0:T(8,128)(2,1)}, bf16[256,256]{1,0:T(8,128)(2,1)}) custom-call(bf16[256,256]{1,0:T(8,128)(2,1)} %get-tuple-element.8.refs_0_, bf16[256,256]{1,0:T(8,128)(2,1)} %get-tuple-element.9.refs_1_, bf16[256,256]{1,0:T(8,128)(2,1)} %get-tuple-element.10.refs_2_, ...), custom_call_target="tpu_custom_call" | custom-call | tf_op jit(solution)/shard_map/pallas_call | solution.py:659
